TPU v7x, 512 devices: a whole 4x8x8 slice. The times are simulated.
512 devices in a mesh: leaf: 64 (over x, z, core), head: 8 (over y).
Axes of the slice: x: 4, y: 8, z: 8, core: 2. Of those that a mesh axis runs over, the one named last changes fastest.
Arguments:
- queries: bfloat16 [2, 4096, 8192], P(None, 'leaf', 'head'), may hold values from -64 to 64
- keys: bfloat16 [2, 4096, 1024], P(None, 'leaf', 'head'), may hold values from -64 to 64
- values: bfloat16 [2, 4096, 1024], P(None, 'leaf', 'head'), may hold values from -6 to 6
- output_gradient: bfloat16 [2, 4096, 8192], P(None, 'leaf', 'head'), may hold values from -6 to 6
- q_gain: float32 [128], replicated, may hold values from 0.5 to 6
- k_gain: float32 [128], replicated, may hold values from 0.5 to 6
- leaf_len: int32 [64], P('leaf'), may hold values from 16 to 64, as said below
Outputs:
- dq: bfloat16 [2, 4096, 8192], P(None, 'leaf', 'head')
- dk: bfloat16 [2, 4096, 1024], P(None, 'leaf', 'head')
- dv: bfloat16 [2, 4096, 1024], P(None, 'leaf', 'head')
- dq_gain: float32 [128], replicated
- dk_gain: float32 [128], replicated
Inputs may be any that keep to these rules, and one draw needn't show every extreme that they name: `leaf_len`: at least one leaf is full (64 live tokens).
All inputs are finite; a program needn't handle non-finite values.
Results may differ from a plain program's by a relative error of at most 0.039.
The roundings to bfloat16 on the way count: a program that leaves them out, or rounds other values in their place, can miss the bound.
Values may be sent and summed in bfloat16 or wider, within the bound.
A program may use at most 64 MiB of HBM per device.

v0:
```python
from functools import reduce

import jax
import jax.numpy as jnp
from jax import lax
from jax.sharding import PartitionSpec as P

NEG_BIG = -1000000000.0
NORM_EPS = 1e-06
ROPE_BASE = 1000000.0


def as_sent(x):

    def short(part):
        return part.astype(jnp.bfloat16) if part.dtype == jnp.float32 else part

    return jax.tree.map(short, x)


def partner(x, axis, apart):
    return lax.ppermute(x, axis, [(i, i ^ 1 << apart) for i in range(lax.axis_size(axis))])


def rotate(values_in, positions, direction):
    half_width = values_in.shape[-1] // 2
    frequency = ROPE_BASE ** (
        -(jnp.arange(half_width, dtype=jnp.float32) * 2.0 / values_in.shape[-1])
    )
    angles = positions.astype(jnp.float32)[..., None] * frequency
    extra_dims = values_in.ndim - 1 - positions.ndim
    angles = angles.reshape(positions.shape + (1,) * extra_dims + (half_width,))
    cosine = jnp.cos(angles)
    sine_part = direction * jnp.sin(angles)
    lower_half = values_in[..., :half_width]
    upper_half = values_in[..., half_width:]
    return jnp.concatenate(
        [
            lower_half * cosine - upper_half * sine_part,
            upper_half * cosine + lower_half * sine_part,
        ],
        axis=-1,
    )


def normalize(values_in, gain_vec):
    mean_square = jnp.mean(values_in * values_in, axis=-1, keepdims=True)
    factor = lax.rsqrt(mean_square + NORM_EPS)
    unit_rows = values_in * factor
    return (unit_rows * gain_vec, unit_rows, factor)


def norm_back(upstream, unit_rows, factor, gain_vec):
    scaled = upstream * gain_vec
    inner_sum = jnp.mean(scaled * unit_rows, axis=-1, keepdims=True)
    gain_grad = jnp.sum((upstream * unit_rows).reshape(-1, upstream.shape[-1]), axis=0)
    return (factor * (scaled - unit_rows * inner_sum), gain_grad)


def on_device(queries, keys, values, output_gradient, q_gain, k_gain, leaf_len):
    leaves_count = lax.axis_size("leaf")
    rollout_depth = leaves_count.bit_length() - 1
    leaf_position_index = lax.axis_index("leaf")
    segment_length = queries.shape[1]
    head_width = q_gain.shape[0]
    kv_heads = keys.shape[2] // head_width
    query_group_count = queries.shape[2] // keys.shape[2]
    score_scale = head_width ** (-0.5)
    hosted = jnp.int32(1)
    for tree_level in range(1, rollout_depth + 1):
        hosted = hosted + (leaf_position_index % 2**tree_level == 0).astype(jnp.int32)
    row_ids = jnp.arange(segment_length, dtype=jnp.int32)
    positions = jnp.stack(
        [
            rollout_depth * segment_length + row_ids,
            jnp.maximum(rollout_depth - hosted, 0) * segment_length + row_ids,
        ]
    )
    query_input = queries.astype(jnp.float32).reshape(
        2, segment_length, kv_heads, query_group_count, head_width
    )
    q_normed, q_unit, q_factor = normalize(query_input, q_gain)
    q_rot = rotate(q_normed, positions, 1.0).astype(jnp.bfloat16)
    key_input = keys.astype(jnp.float32).reshape(2, segment_length, kv_heads, head_width)
    k_normed, k_unit, k_factor = normalize(key_input, k_gain)
    key_rotary = rotate(k_normed, positions, 1.0).astype(jnp.bfloat16)
    tree_levels = jnp.arange(1, rollout_depth + 1, dtype=jnp.int32)
    host_keys = key_rotary[1].reshape(segment_length, kv_heads * head_width)
    host_values = values[1]
    every_k, every_v = (
        lax.all_gather(host_keys[None], "leaf", axis=0, tiled=True),
        lax.all_gather(host_values[None], "leaf", axis=0, tiled=True),
    )
    span_sizes = 2**tree_levels
    owners = leaf_position_index // span_sizes * span_sizes + span_sizes // 2
    chain_k = jnp.take(every_k, owners, axis=0)
    chain_v = jnp.take(every_v, owners, axis=0)
    chain_k = chain_k.reshape(rollout_depth, segment_length, kv_heads, head_width)
    chain_v = chain_v.reshape(rollout_depth, segment_length, kv_heads, head_width)
    slot_keys = [key_rotary[0]] + [chain_k[slot] for slot in range(rollout_depth)]
    slot_values = [values[0].reshape(segment_length, kv_heads, head_width)] + [
        chain_v[slot] for slot in range(rollout_depth)
    ]
    query_rows = q_rot.reshape(2 * segment_length, kv_heads, query_group_count, head_width)
    row_index = jnp.arange(2 * segment_length, dtype=jnp.int32)
    is_leaf = row_index < segment_length
    row_in_slot = row_index % segment_length
    retained_rows = jnp.where(is_leaf, row_in_slot < leaf_len[0], hosted <= rollout_depth)
    output_gradient_rows = jnp.where(
        retained_rows[:, None, None, None],
        output_gradient.reshape(2 * segment_length, kv_heads, query_group_count, head_width),
        jnp.zeros((), jnp.bfloat16),
    )
    causal = row_ids[None, :] <= row_in_slot[:, None]
    slot_masks = [is_leaf[:, None] & causal & (row_ids[None, :] < leaf_len[0])]
    for tree_level in range(1, rollout_depth + 1):
        slot_masks.append(
            is_leaf[:, None] | (tree_level > hosted) | (tree_level == hosted) & causal
        )
    scores = []
    for slot in range(rollout_depth + 1):
        score = (
            jnp.einsum(
                "rkgd,skd->kgrs", query_rows, slot_keys[slot], preferred_element_type=jnp.float32
            )
            * score_scale
        )
        scores.append(jnp.where(slot_masks[slot], score, NEG_BIG))
    row_top = reduce(jnp.maximum, [jnp.max(score, axis=-1) for score in scores])[..., None]
    exp_total = reduce(jnp.add, [jnp.sum(jnp.exp(score - row_top), axis=-1) for score in scores])[
        ..., None
    ]
    log_total = row_top + jnp.log(exp_total)
    probs = []
    probs_low = []
    dprobs = []
    delta_sum = jnp.zeros(row_top.shape[:-1], jnp.float32)
    for slot in range(rollout_depth + 1):
        prob = jnp.exp(scores[slot] - log_total)
        prob_low = prob.astype(jnp.bfloat16)
        dprob = jnp.einsum(
            "rkgd,skd->kgrs",
            output_gradient_rows,
            slot_values[slot],
            preferred_element_type=jnp.float32,
        )
        delta_sum = delta_sum + jnp.sum(prob_low.astype(jnp.float32) * dprob, axis=-1)
        probs.append(prob)
        probs_low.append(prob_low)
        dprobs.append(dprob)
    query_rotary_gradient = jnp.zeros(query_rows.shape, jnp.float32)
    dk_slots = []
    dv_slots = []
    for slot in range(rollout_depth + 1):
        dscore = (probs[slot] * (dprobs[slot] - delta_sum[..., None])).astype(jnp.bfloat16)
        query_rotary_gradient = (
            query_rotary_gradient
            + jnp.einsum(
                "kgrs,skd->rkgd", dscore, slot_keys[slot], preferred_element_type=jnp.float32
            )
            * score_scale
        )
        dk_slots.append(
            jnp.einsum("kgrs,rkgd->skd", dscore, query_rows, preferred_element_type=jnp.float32)
            * score_scale
        )
        dv_slots.append(
            jnp.einsum(
                "kgrs,rkgd->skd",
                probs_low[slot],
                output_gradient_rows,
                preferred_element_type=jnp.float32,
            )
        )
    chain_dk = jnp.stack(dk_slots[1:]).reshape(rollout_depth, segment_length, kv_heads * head_width)
    chain_dv = jnp.stack(dv_slots[1:]).reshape(rollout_depth, segment_length, kv_heads * head_width)
    for bit_index in range(rollout_depth):
        got_dk, got_dv = partner(
            (as_sent(chain_dk[bit_index:]), as_sent(chain_dv[bit_index:])), "leaf", bit_index
        )
        chain_dk = jnp.concatenate([chain_dk[:bit_index], chain_dk[bit_index:] + got_dk], axis=0)
        chain_dv = jnp.concatenate([chain_dv[:bit_index], chain_dv[bit_index:] + got_dv], axis=0)
    pick_slot = jnp.clip(hosted - 1, 0, rollout_depth - 1)
    own_node = hosted <= rollout_depth
    node_dk = jnp.where(
        own_node, lax.dynamic_index_in_dim(chain_dk, pick_slot, 0, keepdims=False), 0.0
    )
    node_dv = jnp.where(
        own_node, lax.dynamic_index_in_dim(chain_dv, pick_slot, 0, keepdims=False), 0.0
    )
    dk_rot = jnp.stack([dk_slots[0], node_dk.reshape(segment_length, kv_heads, head_width)])
    value_gradient_total = jnp.stack(
        [dv_slots[0], node_dv.reshape(segment_length, kv_heads, head_width)]
    )
    q_back = rotate(
        query_rotary_gradient.reshape(2, segment_length, kv_heads, query_group_count, head_width),
        positions,
        -1.0,
    )
    dq_in, dq_part = norm_back(q_back, q_unit, q_factor, q_gain)
    k_back = rotate(dk_rot, positions, -1.0)
    key_input_gradient, dk_part = norm_back(k_back, k_unit, k_factor, k_gain)
    dq_gain, dk_gain = lax.psum((dq_part, dk_part), ("leaf", "head"))
    dq = dq_in.astype(jnp.bfloat16).reshape(queries.shape)
    dk = key_input_gradient.astype(jnp.bfloat16).reshape(keys.shape)
    dv = value_gradient_total.astype(jnp.bfloat16).reshape(values.shape)
    return (dq, dk, dv, dq_gain, dk_gain)


def solution(mesh):
    return jax.shard_map(
        on_device,
        mesh=mesh,
        in_specs=(
            P(None, "leaf", "head"),
            P(None, "leaf", "head"),
            P(None, "leaf", "head"),
            P(None, "leaf", "head"),
            P(),
            P(),
            P("leaf"),
        ),
        out_specs=(
            P(None, "leaf", "head"),
            P(None, "leaf", "head"),
            P(None, "leaf", "head"),
            P(),
            P(),
        ),
        check_vma=False,
    )
```

profile of v0, /device:TPU:1, one launch (start us, length us, event | category | flops | bytes accessed | tf_op | source)
XLA Modules:
  0.0 356.0 jit_solution(11428059105833602047)
XLA Ops:
  11.1 0.9 broadcast_multiply_fusion
  16.4 0.9 mul.623
  18.3 81.5 %all-gather.6.cloned.1.call-done = bf16[64,64,1,128]{3,1,2,0:T(8,128)(2,1)} async-done(((bf16[1,64,1,128]{3,1,2,0:T(8,128)(2,1)}), bf16[64,64,1,128]{3,1,2,0:T(8,128)(2,1)}) %all-gather.6.cloned.1.call-update) | async-done | bytes 1048592 | tf_op jit(solution)/shard_map/all_gather | solution.py:91
  99.8 1.8 gather_fusion
  101.6 81.3 %all-gather.4.cloned.1.call-done = bf16[64,64,128]{2,1,0:T(8,128)(2,1)} async-done(((bf16[1,64,128]{2,1,0:T(8,128)(2,1)}), bf16[64,64,128]{2,1,0:T(8,128)(2,1)}) %all-gather.4.cloned.1.call-update) | async-done | bytes 1048592 | tf_op jit(solution)/shard_map/all_gather | solution.py:92
  182.9 1.8 gather_fusion.1
  194.8 2.1 collective-permute-start
  198.9 2.2 collective-permute-start.6
  204.0 0.9 concatenate.112
  208.1 1.0 bitcast_add_fusion.1
  209.1 2.4 collective-permute-start.1
  211.5 0.9 bitcast_add_fusion
  212.4 2.9 collective-permute-start.7
  215.4 3.7 %collective-permute-start.2 = (bf16[4,64,128]{2,1,0:T(8,128)(2,1)S(1)}, bf16[4,64,128]{2,1,0:T(8,128)(2,1)S(1)}, u32[]{:S(2)}, u32[]{:S(2)}) collective-permute-start(bf16[4,64,128]{2,1,0:T(8,128)(2,1)S(1)} %slice.327), channel_id=1, source_target_pairs={{0,32},{8,40},{16,48},{24,56},{32,0},{40,8},{48,16},{56,24},{64,96... | collective-permute-start | bytes 196616 | tf_op jit(solution)/shard_map/ppermute | solution.py:22
  219.1 2.5 collective-permute-start.8
  221.7 1.5 collective-permute-done.2
  223.2 4.6 %collective-permute-start.3 = (bf16[3,64,128]{2,1,0:T(8,128)(2,1)S(1)}, bf16[3,64,128]{2,1,0:T(8,128)(2,1)S(1)}, u32[]{:S(2)}, u32[]{:S(2)}) collective-permute-start(bf16[3,64,128]{2,1,0:T(8,128)(2,1)S(1)} %slice.329), channel_id=1, source_target_pairs={{0,64},{8,72},{16,80},{24,88},{32,96},{40,104},{48,112},{56,120},{... | collective-permute-start | bytes 147464 | tf_op jit(solution)/shard_map/ppermute | solution.py:22
  227.9 4.6 %collective-permute-start.9 = (bf16[3,64,128]{2,1,0:T(8,128)(2,1)S(1)}, bf16[3,64,128]{2,1,0:T(8,128)(2,1)S(1)}, u32[]{:S(2)}, u32[]{:S(2)}) collective-permute-start(bf16[3,64,128]{2,1,0:T(8,128)(2,1)S(1)} %get-tuple-element.35), channel_id=1, source_target_pairs={{0,64},{8,72},{16,80},{24,88},{32,96},{40,104},{48,112},{56,120},{... | collective-permute-start | bytes 147464 | tf_op jit(solution)/shard_map/ppermute | solution.py:22
  232.6 2.2 collective-permute-start.4
  234.8 1.9 collective-permute-done.9
  236.7 1.9 collective-permute-start.10
  238.6 3.1 collective-permute-start.5
  241.9 3.6 %collective-permute-start.11 = (bf16[1,64,128]{2,1,0:T(8,128)(2,1)S(1)}, bf16[1,64,128]{2,1,0:T(8,128)(2,1)S(1)}, u32[]{:S(2)}, u32[]{:S(2)}) collective-permute-start(bf16[1,64,128]{2,1,0:T(8,128)(2,1)S(1)} %slice.332), channel_id=1, source_target_pairs={{0,256},{8,264},{16,272},{24,280},{32,288},{40,296},{48,304},{56,3... | collective-permute-start | bytes 49160 | tf_op jit(solution)/shard_map/ppermute | solution.py:22
  248.2 99.6 %all-reduce = (f32[128]{0:T(128)}, f32[128]{0:T(128)}) all-reduce(f32[128]{0:T(128)S(1)} %fusion.43, f32[128]{0:T(128)S(1)} %get-tuple-element.6), channel_id=1, replica_groups=mesh['leaf'=64,'head'=8] {'leaf','head'}, use_global_device_ids=true, to_apply=%region_26.28 | all-reduce | flops 256 | bytes 2048 | tf_op jit(solution)/shard_map/psum | solution.py:203
  (195 shorter events, 30.3 us)
Async XLA Ops:
  7.2 92.6 %all-gather.6.cloned.1.call-start = ((), (), s32[]{:S(2)}) async-start(), calls=%async_computation.1 | async-start | bytes 1064960 | tf_op jit(solution)/shard_map/all_gather | solution.py:91
  7.3 3.8 %copy-start.22 = (f32[64]{0:T(128)}, f32[64]{0:T(128)S(1)}, u32[]{:S(2)}) copy-start(f32[64]{0:T(128)S(1)} %negate_power_fusion) | copy-start | bytes 772
  9.2 8.8 %copy-start.12 = (bf16[2,64,1,64]{3,1,2,0:T(8,128)(2,1)}, bf16[2,64,1,64]{3,1,2,0:T(8,128)(2,1)S(1)}, u32[]{:S(2)}) copy-start(bf16[2,64,1,64]{3,1,2,0:T(8,128)(2,1)S(1)} %fusion.118) | copy-start | bytes 49156
  9.6 8.4 %copy-start.14 = (bf16[2,64,1,64]{3,1,2,0:T(8,128)(2,1)}, bf16[2,64,1,64]{3,1,2,0:T(8,128)(2,1)S(1)}, u32[]{:S(2)}) copy-start(bf16[2,64,1,64]{3,1,2,0:T(8,128)(2,1)S(1)} %fusion.91) | copy-start | bytes 49156
  10.3 172.6 %all-gather.4.cloned.1.call-start = ((), (), s32[]{:S(2)}) async-start(), calls=%async_computation | async-start | bytes 1064960 | tf_op jit(solution)/shard_map/all_gather | solution.py:92
  17.3 171.2 %copy-start.28 = (pred[128]{0:T(512)(128)(4,1)}, pred[128]{0:T(512)(128)(4,1)S(1)}, u32[]{:S(2)}) copy-start(pred[128]{0:T(512)(128)(4,1)S(1)} %compare_select_fusion.1) | copy-start | bytes 388
  194.1 3.1 copy-start.8
  194.8 12.6 %collective-permute-start = (bf16[6,64,128]{2,1,0:T(8,128)(2,1)}, bf16[6,64,128]{2,1,0:T(8,128)(2,1)}, u32[]{:S(2)}, u32[]{:S(2)}) collective-permute-start(bf16[6,64,128]{2,1,0:T(8,128)(2,1)} %bitcast_convert_fusion.1), channel_id=1, source_target_pairs={{0,8},{8,0},{16,24},{24,16},{32,40},{40,32},{48,56},{56,48},{64,72... | collective-permute-start | bytes 294920 | tf_op jit(solution)/shard_map/ppermute | solution.py:22
  198.2 3.5 copy-start.10
  198.2 2.9 copy-start.18
  198.9 12.6 %collective-permute-start.6 = (bf16[6,64,128]{2,1,0:T(8,128)(2,1)}, bf16[6,64,128]{2,1,0:T(8,128)(2,1)}, u32[]{:S(2)}, u32[]{:S(2)}) collective-permute-start(bf16[6,64,128]{2,1,0:T(8,128)(2,1)} %bitcast_convert_fusion), channel_id=1, source_target_pairs={{0,8},{8,0},{16,24},{24,16},{32,40},{40,32},{48,56},{56,48},{64,72... | collective-permute-start | bytes 294920 | tf_op jit(solution)/shard_map/ppermute | solution.py:22
  208.1 3.4 copy-start.11
  209.0 6.3 %copy-start.6 = (f32[6,64,128]{2,1,0:T(8,128)}, f32[6,64,128]{2,1,0:T(8,128)S(1)}, u32[]{:S(2)}) copy-start(f32[6,64,128]{2,1,0:T(8,128)S(1)} %bitcast_add_fusion.1) | copy-start | bytes 589828
  209.1 6.3 %collective-permute-start.1 = (bf16[5,64,128]{2,1,0:T(8,128)(2,1)S(1)}, bf16[5,64,128]{2,1,0:T(8,128)(2,1)S(1)}, u32[]{:S(2)}, u32[]{:S(2)}) collective-permute-start(bf16[5,64,128]{2,1,0:T(8,128)(2,1)S(1)} %slice.325), channel_id=1, source_target_pairs={{0,16},{8,24},{16,0},{24,8},{32,48},{40,56},{48,32},{56,40},{64,80... | collective-permute-start | bytes 245768 | tf_op jit(solution)/shard_map/ppermute | solution.py:22
  212.4 6.6 %collective-permute-start.7 = (bf16[5,64,128]{2,1,0:T(8,128)(2,1)S(1)}, bf16[5,64,128]{2,1,0:T(8,128)(2,1)S(1)}, u32[]{:S(2)}, u32[]{:S(2)}) collective-permute-start(bf16[5,64,128]{2,1,0:T(8,128)(2,1)S(1)} %slice.324), channel_id=1, source_target_pairs={{0,16},{8,24},{16,0},{24,8},{32,48},{40,56},{48,32},{56,40},{64,80... | collective-permute-start | bytes 245768 | tf_op jit(solution)/shard_map/ppermute | solution.py:22
  215.4 7.8 %collective-permute-start.2 = (bf16[4,64,128]{2,1,0:T(8,128)(2,1)S(1)}, bf16[4,64,128]{2,1,0:T(8,128)(2,1)S(1)}, u32[]{:S(2)}, u32[]{:S(2)}) collective-permute-start(bf16[4,64,128]{2,1,0:T(8,128)(2,1)S(1)} %slice.327), channel_id=1, source_target_pairs={{0,32},{8,40},{16,48},{24,56},{32,0},{40,8},{48,16},{56,24},{64,96... | collective-permute-start | bytes 196616 | tf_op jit(solution)/shard_map/ppermute | solution.py:22
  219.1 8.7 %collective-permute-start.8 = (bf16[4,64,128]{2,1,0:T(8,128)(2,1)S(1)}, bf16[4,64,128]{2,1,0:T(8,128)(2,1)S(1)}, u32[]{:S(2)}, u32[]{:S(2)}) collective-permute-start(bf16[4,64,128]{2,1,0:T(8,128)(2,1)S(1)} %slice.326), channel_id=1, source_target_pairs={{0,32},{8,40},{16,48},{24,56},{32,0},{40,8},{48,16},{56,24},{64,96... | collective-permute-start | bytes 196616 | tf_op jit(solution)/shard_map/ppermute | solution.py:22
  223.2 9.4 %collective-permute-start.3 = (bf16[3,64,128]{2,1,0:T(8,128)(2,1)S(1)}, bf16[3,64,128]{2,1,0:T(8,128)(2,1)S(1)}, u32[]{:S(2)}, u32[]{:S(2)}) collective-permute-start(bf16[3,64,128]{2,1,0:T(8,128)(2,1)S(1)} %slice.329), channel_id=1, source_target_pairs={{0,64},{8,72},{16,80},{24,88},{32,96},{40,104},{48,112},{56,120},{... | collective-permute-start | bytes 147464 | tf_op jit(solution)/shard_map/ppermute | solution.py:22
  227.8 4.7 %slice-start = ((f32[6,64,128]{2,1,0:T(8,128)}), f32[1,64,128]{2,1,0:T(8,128)S(1)}, s32[]{:S(2)}) async-start(f32[6,64,128]{2,1,0:T(8,128)} %copy-done.6), calls=%async_computation.2 | async-start | bytes 65536 | tf_op jit(solution)/shard_map/slice | solution.py:181
  227.9 8.8 %collective-permute-start.9 = (bf16[3,64,128]{2,1,0:T(8,128)(2,1)S(1)}, bf16[3,64,128]{2,1,0:T(8,128)(2,1)S(1)}, u32[]{:S(2)}, u32[]{:S(2)}) collective-permute-start(bf16[3,64,128]{2,1,0:T(8,128)(2,1)S(1)} %get-tuple-element.35), channel_id=1, source_target_pairs={{0,64},{8,72},{16,80},{24,88},{32,96},{40,104},{48,112},{56,120},{... | collective-permute-start | bytes 147464 | tf_op jit(solution)/shard_map/ppermute | solution.py:22
  232.6 6.0 %collective-permute-start.4 = (bf16[2,64,128]{2,1,0:T(8,128)(2,1)S(1)}, bf16[2,64,128]{2,1,0:T(8,128)(2,1)S(1)}, u32[]{:S(2)}, u32[]{:S(2)}) collective-permute-start(bf16[2,64,128]{2,1,0:T(8,128)(2,1)S(1)} %slice.331), channel_id=1, source_target_pairs={{0,128},{8,136},{16,144},{24,152},{32,160},{40,168},{48,176},{56,1... | collective-permute-start | bytes 98312 | tf_op jit(solution)/shard_map/ppermute | solution.py:22
  236.7 5.1 %collective-permute-start.10 = (bf16[2,64,128]{2,1,0:T(8,128)(2,1)S(1)}, bf16[2,64,128]{2,1,0:T(8,128)(2,1)S(1)}, u32[]{:S(2)}, u32[]{:S(2)}) collective-permute-start(bf16[2,64,128]{2,1,0:T(8,128)(2,1)S(1)} %slice.330), channel_id=1, source_target_pairs={{0,128},{8,136},{16,144},{24,152},{32,160},{40,168},{48,176},{56,1... | collective-permute-start | bytes 98312 | tf_op jit(solution)/shard_map/ppermute | solution.py:22
  238.6 6.9 %collective-permute-start.5 = (bf16[1,64,128]{2,1,0:T(8,128)(2,1)S(1)}, bf16[1,64,128]{2,1,0:T(8,128)(2,1)S(1)}, u32[]{:S(2)}, u32[]{:S(2)}) collective-permute-start(bf16[1,64,128]{2,1,0:T(8,128)(2,1)S(1)} %slice.333), channel_id=1, source_target_pairs={{0,256},{8,264},{16,272},{24,280},{32,288},{40,296},{48,304},{56,3... | collective-permute-start | bytes 49160 | tf_op jit(solution)/shard_map/ppermute | solution.py:22
  241.9 105.9 %collective-permute-start.11 = (bf16[1,64,128]{2,1,0:T(8,128)(2,1)S(1)}, bf16[1,64,128]{2,1,0:T(8,128)(2,1)S(1)}, u32[]{:S(2)}, u32[]{:S(2)}) collective-permute-start(bf16[1,64,128]{2,1,0:T(8,128)(2,1)S(1)} %slice.332), channel_id=1, source_target_pairs={{0,256},{8,264},{16,272},{24,280},{32,288},{40,296},{48,304},{56,3... | collective-permute-start | bytes 49160 | tf_op jit(solution)/shard_map/ppermute | solution.py:22
  (21 other events, 22.1 us)
Sparse Core Ops, SparseCore 0:
  11.4 88.3 all-gather.5
  103.2 79.7 all-gather.3
where the time goes:
time: 357 us; the launch traced here: 356 us
  waiting for transfers between devices  166 us (46%)
  blocking collectives  99.6 us (28%)
  starting transfers between devices  35.9 us (10%)
  local copies, waits for them, and re-layouts  16.5 us (5%)
  between operations  15.9 us (4%)
  other arithmetic  12.7 us (4%)
  matrix products  8.95 us (3%)
    psum x1, blocking collectives, on_device(): dq_gain, dk_gain = lax.psum((dq_part, dk_part), ('leaf', 'head'))  99.6 us
    all_gather x1, waiting for transfers between devices, on_device(): lax.all_gather(host_keys[None], 'leaf', axis=0, tiled=True)  81.5 us
    all_gather x1, waiting for transfers between devices, on_device(): lax.all_gather(host_values[None], 'leaf', axis=0, tiled=True)  81.3 us
    ppermute x12, starting transfers between devices, partner(): lax.ppermute(x, axis, [(i, i ^ 1 << apart) for i in range(lax.axis_size(a...  35.9 us
    unnamed x63, local copies, waits for them, and re-layouts  8.71 us
  transfers between devices with their start and end apart: 14, of which 5 were waited for; matrix products, arithmetic and copies ran while one was open for 5% of the time, Pallas kernels for 0%

commit v1 on v0

v1 whole, which is shorter than its diff:
```python
import jax
import jax.numpy as jnp
import numpy as np
from jax import lax
from jax.experimental import pallas as pl
from jax.experimental.pallas import tpu as pltpu
from jax.sharding import PartitionSpec as P

NEG_BIG = -1000000000.0
NORM_EPS = 1e-06
ROPE_BASE = 1000000.0
DEPTH = 6
T = 64
D = 128
G = 8
SLOTS = DEPTH + 1
KEYS = SLOTS * T
ROWS = G * T
NX, NZ, NC, NY = 4, 8, 2, 8
NQ = NZ * NC
SCALE = D ** (-0.5)
BF = jnp.bfloat16
F32 = jnp.float32
MESH = pl.DeviceIdType.MESH


def rope_table():
    frequency = (ROPE_BASE ** (-(np.arange(D // 2, dtype=np.float32) * 2.0 / D))).astype(np.float32)
    angles = np.arange(KEYS, dtype=np.float32)[:, None] * frequency
    return np.concatenate([np.cos(angles), np.sin(angles)], axis=1).astype(np.float32)


def spread(table):
    lane = lax.broadcasted_iota(jnp.int32, table.shape, 1)
    other = pltpu.roll(table, D // 2, axis=1)
    low = lane < D // 2
    return jnp.where(low, table, other), jnp.where(low, -other, table)


def turn(x, cosine, sine):
    return x * cosine + pltpu.roll(x, D // 2, axis=1) * sine


def unturn(x, cosine, sine):
    return x * cosine - pltpu.roll(x, D // 2, axis=1) * sine


def unit_of(x):
    factor = lax.rsqrt(jnp.mean(x * x, axis=-1, keepdims=True) + NORM_EPS)
    return x * factor, factor


def dot(a, b, contract):
    return lax.dot_general(a, b, (contract, ((), ())), preferred_element_type=F32)


def kernel(
    q_in, k_in, v_in, g_in, qg_in, kg_in, len_in, table_in,
    dq_out, dk_out, dv_out, dqg_out, dkg_out,
    q_raw, g_raw, own, kv, qg, kg, length, table,
    q_rot, q_unit, g_rows, k_rot, k_unit, v_all, part, y_q, dq_buf, dkv_buf,
    send_kv, send_sum, x_recv, z_recv, gain_send, gain_z, gain_x, gain_y, gain_total,
    load_sem, store_sem, b_send, b_recv, r_send, r_recv, x_sem, xr_sem, s_send,
    gz_send, gz_recv, gx_send, gx_recv, gy_send, gy_recv,
):
    leaf = lax.axis_index("leaf")
    y = lax.axis_index("head")
    x = leaf // NQ
    q = lax.rem(leaf, NQ)
    z = q // NC
    c = lax.rem(q, NC)

    def at(xx, qq, yy=None):
        return (xx * NQ + qq, y if yy is None else yy)

    hosted = jnp.int32(1)
    for level in range(1, DEPTH + 1):
        hosted = hosted + jnp.where(lax.rem(leaf, 2**level) == 0, 1, 0)

    def remote(src, dst, send, recv, device):
        return pltpu.make_async_remote_copy(
            src_ref=src, dst_ref=dst, send_sem=send, recv_sem=recv, device_id=device, device_id_type=MESH
        )

    holder = {level: q // 2**level * 2**level + 2 ** (level - 1) for level in range(1, 5)}
    is_relay = q == 1
    far_owner = jnp.logical_and(q == 0, x > 0)

    loads = [
        pltpu.make_async_copy(k_in.at[1], own.at[0], load_sem.at[0]),
        pltpu.make_async_copy(v_in.at[1], own.at[1], load_sem.at[1]),
        pltpu.make_async_copy(k_in.at[0], kv.at[0, 0], load_sem.at[2]),
        pltpu.make_async_copy(v_in.at[0], kv.at[0, 1], load_sem.at[3]),
        pltpu.make_async_copy(table_in, table, load_sem.at[4]),
        pltpu.make_async_copy(qg_in, qg, load_sem.at[5]),
        pltpu.make_async_copy(kg_in, kg, load_sem.at[6]),
        pltpu.make_async_copy(q_in, q_raw, load_sem.at[7]),
        pltpu.make_async_copy(g_in, g_raw, load_sem.at[8]),
        pltpu.make_async_copy(len_in, length, load_sem.at[9]),
    ]
    for load in loads:
        load.start()

    barrier = pltpu.get_barrier_semaphore()

    def greet(device):
        pl.semaphore_signal(barrier, inc=1, device_id=device, device_id_type=MESH)

    @pl.when(is_relay)
    def _():
        greet(at(2, 0))
        greet(at(x // 2 * 2 + 1, 0))

    for other in range(1, NX):
        greet(at(lax.rem(x + other, NX), q))

    @pl.when(jnp.logical_not(is_relay))
    def _():
        greet(at(x, 1))

    for level in (4, 3, 2, 1):

        @pl.when(q != holder[level])
        def _(level=level):
            greet(at(x, holder[level]))

    for other in range(1, NY):
        greet(at(x, z * NC + 1, lax.rem(y + other, NY)))

    early = jnp.int32(NX - 1)
    early = early + jnp.where(c == 1, 1 + (NY - 1) * NC, 0)
    early = early + jnp.where(is_relay, NQ - 1, 0)
    for level in (2, 3, 4):
        early = early + jnp.where(hosted == level, 2**level - 1, 0)
    early = early + jnp.where(hosted == 5, 2, 0) + jnp.where(hosted == 6, NX, 0)

    loads[0].wait()
    loads[1].wait()

    @pl.when(far_owner)
    def _():
        pl.semaphore_wait(barrier, early)

        @pl.when(x == 2)
        def _():
            for xx in range(NX):
                remote(own, kv.at[6], b_send.at[xx], b_recv.at[6], at(xx, 1)).start()

        @pl.when(x != 2)
        def _():
            for n in range(2):
                remote(own, kv.at[5], b_send.at[n], b_recv.at[5], at(x - n, 1)).start()

    @pl.when(jnp.logical_not(far_owner))
    def _():
        pl.semaphore_wait(barrier, early)

    for level in (4, 3, 2, 1):

        @pl.when(hosted == level)
        def _(level=level):
            half = 2 ** (level - 1)
            offsets = sorted((o for o in range(-half, half) if o), key=lambda o: -abs(o))
            for n, offset in enumerate(offsets):
                remote(own, kv.at[level], b_send.at[n], b_recv.at[level], at(x, q + offset)).start()
            for n in range(2):
                pltpu.make_async_copy((k_in, v_in)[n].at[1], kv.at[level, n], load_sem.at[10 + n]).start()

    others = [qq for zz in (4, 3, 5, 2, 6, 1, 7, 0) for qq in (2 * zz, 2 * zz + 1) if qq != 1]

    @pl.when(is_relay)
    def _():
        for level in (5, 6):
            remote(own, kv.at[level], b_send.at[0], b_recv.at[level], at(x, 0)).wait_recv()
            for n, qq in enumerate(others):
                remote(
                    kv.at[level], kv.at[level], b_send.at[1 + (level - 5) * 15 + n], b_recv.at[level], at(x, qq)
                ).start()

    for load in loads[4:]:
        load.wait()
    q_gain, k_gain = qg[...], kg[...]
    place = [DEPTH * T, jnp.maximum(DEPTH - hosted, 0) * T]
    live = [
        lax.broadcasted_iota(jnp.int32, (T, D), 0) < length[0],
        jnp.broadcast_to(hosted <= DEPTH, (T, D)),
    ]
    for kind in range(2):
        cosine, sine = spread(table[pl.ds(pl.multiple_of(place[kind], T), T), :])
        for head in range(G):
            rows = pl.ds(kind * ROWS + head * T, T)
            unit, _ = unit_of(q_raw[kind, :, head * D : (head + 1) * D].astype(F32))
            q_unit[rows, :] = unit
            q_rot[rows, :] = turn(unit * q_gain, cosine, sine).astype(BF)
            grad = g_raw[kind, :, head * D : (head + 1) * D]
            g_rows[rows, :] = jnp.where(live[kind], grad, jnp.zeros((), BF))

    loads[2].wait()
    loads[3].wait()

    def take(slot):
        rows = pl.ds(slot * T, T)
        cosine, sine = spread(table[(DEPTH - slot) * T : (DEPTH - slot + 1) * T, :])
        unit, _ = unit_of(kv[slot, 0].astype(F32))
        k_unit[rows, :] = unit
        k_rot[rows, :] = turn(unit * k_gain, cosine, sine).astype(BF)
        v_all[rows, :] = kv[slot, 1]

    take(0)
    for level in range(1, 5):

        @pl.when(q != holder[level])
        def _(level=level):
            remote(own, kv.at[level], b_send.at[0], b_recv.at[level], at(x, holder[level])).wait_recv()

        @pl.when(hosted == level)
        def _(level=level):
            for n in range(2):
                pltpu.make_async_copy((k_in, v_in)[n].at[1], kv.at[level, n], load_sem.at[10 + n]).wait()

        take(level)

    @pl.when(jnp.logical_not(is_relay))
    def _():
        for level in (5, 6):
            remote(own, kv.at[level], b_send.at[0], b_recv.at[level], at(x, 1)).wait_recv()

    take(5)
    take(6)

    key_at = lax.broadcasted_iota(jnp.int32, (T, ROWS), 0)
    row_at = lax.rem(lax.broadcasted_iota(jnp.int32, (T, ROWS), 1), T)
    ahead = key_at - row_at
    dk = dv = None
    for kind in range(2):
        rows = slice(kind * ROWS, (kind + 1) * ROWS)
        first = 0 if kind == 0 else T
        keys, vals = k_rot[first:, :], v_all[first:, :]
        queries, grads = q_rot[rows, :], g_rows[rows, :]
        scores = dot(keys, queries, ((1,), (1,))) * SCALE
        pieces = []
        for slot in range(SLOTS):
            if kind == 0:
                piece = scores[slot * T : (slot + 1) * T]
                if slot == 0:
                    seen = jnp.logical_and(ahead <= 0, key_at < length[0])
                    piece = jnp.where(seen, piece, NEG_BIG)
            elif slot == 0:
                continue
            else:
                piece = scores[(slot - 1) * T : slot * T]
                bound = jnp.where(hosted == slot, 0, jnp.where(hosted < slot, T, -T))
                piece = jnp.where(ahead <= bound, piece, NEG_BIG)
            pieces.append(piece)
        scores = jnp.concatenate(pieces, axis=0)
        top = jnp.max(scores, axis=0, keepdims=True)
        raised = jnp.exp(scores - top)
        probs = raised * (1.0 / jnp.sum(raised, axis=0, keepdims=True))
        probs_low = probs.astype(BF)
        dprobs = dot(vals, grads, ((1,), (1,)))
        delta = jnp.sum(probs_low.astype(F32) * dprobs, axis=0, keepdims=True)
        dscores = (probs * (dprobs - delta)).astype(BF)
        dv_part = dot(probs_low, grads, ((1,), (0,)))
        dk_part = dot(dscores, queries, ((1,), (0,))) * SCALE
        dq_turned = dot(keys, dscores, ((0,), (0,))) * SCALE
        y_q[rows, :] = jnp.transpose(dq_turned)
        for slot in range(SLOTS):
            if kind == 1 and slot == 0:
                continue
            here = slice(slot * T - first, (slot + 1) * T - first)
            if kind == 0:
                part[slot, 0] = dk_part[here]
                part[slot, 1] = dv_part[here]
            else:
                part[slot, 0] += dk_part[here]
                part[slot, 1] += dv_part[here]

    for slot in range(1, SLOTS):
        send_kv[slot - 1] = part[slot].astype(BF)

    @pl.when(x != 2)
    def _():
        n = jnp.minimum(x, 2)
        remote(send_kv.at[5], x_recv.at[n], x_sem.at[0], xr_sem.at[n], at(2, q)).start()

    @pl.when(lax.rem(x, 2) == 0)
    def _():
        remote(send_kv.at[4], x_recv.at[3], x_sem.at[1], xr_sem.at[3], at(x + 1, q)).start()

    gain_q = jnp.zeros((1, D), F32)
    for kind in range(2):
        cosine, sine = spread(table[pl.ds(pl.multiple_of(place[kind], T), T), :])
        for head in range(G):
            rows = pl.ds(kind * ROWS + head * T, T)
            back = unturn(y_q[rows, :], cosine, sine)
            y_q[rows, :] = back
            gain_q = gain_q + jnp.sum(back * q_unit[rows, :], axis=0, keepdims=True)
    gain_k = jnp.zeros((1, D), F32)
    for slot in range(SLOTS):
        cosine, sine = spread(table[(DEPTH - slot) * T : (DEPTH - slot + 1) * T, :])
        back = unturn(part[slot, 0], cosine, sine)
        gain_k = gain_k + jnp.sum(back * k_unit[slot * T : (slot + 1) * T, :], axis=0, keepdims=True)
    row = lax.broadcasted_iota(jnp.int32, (8, D), 0)
    terms = jnp.where(row == 0, gain_q, jnp.where(row == 1, gain_k, 0.0))
    gain_send[0] = terms

    for zz in range(NZ):
        qq = 2 * zz + 1

        @pl.when(q != qq)
        def _(zz=zz, qq=qq):
            remote(gain_send.at[0], gain_z.at[q], gz_send.at[zz], gz_recv.at[q], at(x, qq)).start()

    for level in range(1, 5):

        @pl.when(q != holder[level])
        def _(level=level):
            n = lax.rem(q, 2**level)
            remote(send_kv.at[level - 1], z_recv.at[n], r_send.at[level], r_recv.at[n], at(x, holder[level])).start()

    for kind in range(2):
        for head in range(G):
            rows = pl.ds(kind * ROWS + head * T, T)
            columns = slice(head * D, (head + 1) * D)
            raw = q_raw[kind, :, columns].astype(F32)
            unit, factor = unit_of(raw)
            scaled = y_q[rows, :] * q_gain
            inner = jnp.mean(scaled * unit, axis=-1, keepdims=True)
            dq_buf[kind, :, columns] = (factor * (scaled - unit * inner)).astype(BF)
    stores = [pltpu.make_async_copy(dq_buf, dq_out, store_sem.at[0])]
    stores[0].start()

    def key_gradient(raw, turned, start):
        cosine, sine = spread(table[pl.ds(start, T), :])
        unit, factor = unit_of(raw.astype(F32))
        scaled = unturn(turned, cosine, sine) * k_gain
        inner = jnp.mean(scaled * unit, axis=-1, keepdims=True)
        return (factor * (scaled - unit * inner)).astype(BF)

    dkv_buf[0, 0] = key_gradient(kv[0, 0], part[0, 0], DEPTH * T)
    dkv_buf[1, 0] = part[0, 1].astype(BF)

    def from_x(n):
        remote(own, x_recv.at[n], x_sem.at[0], xr_sem.at[n], at(x, q)).wait_recv()

    @pl.when(x == 2)
    def _():
        total = part[6]
        for n in range(3):
            from_x(n)
            total = total + x_recv[n].astype(F32)
        part[6] = total
        send_sum[...] = total.astype(BF)

    @pl.when(lax.rem(x, 2) == 1)
    def _():
        from_x(3)
        total = part[5] + x_recv[3].astype(F32)
        part[5] = total
        send_sum[...] = total.astype(BF)

    @pl.when(jnp.logical_and(x > 0, q != 0))
    def _():
        remote(send_sum, z_recv.at[q], s_send, r_recv.at[q], at(x, 0)).start()

    @pl.when(c == 1)
    def _():
        gain_z[q] = terms
        for zz in range(NZ):
            for cc in range(NC):
                qq = zz * NC + cc

                @pl.when(q != qq)
                def _(qq=qq):
                    remote(gain_send.at[0], gain_z.at[qq], gz_send.at[0], gz_recv.at[qq], at(x, qq)).wait_recv()

        total = gain_z[0]
        for qq in range(1, NQ):
            total = total + gain_z[qq]
        gain_send[1] = total
        gain_x[x] = total
        for other in range(1, NX):
            remote(
                gain_send.at[1], gain_x.at[x], gx_send.at[other], gx_recv.at[x], at(lax.rem(x + other, NX), q)
            ).start()
        for other in range(1, NX):
            xx = lax.rem(x + other, NX)
            remote(gain_send.at[1], gain_x.at[xx], gx_send.at[other], gx_recv.at[xx], at(xx, q)).wait_recv()
        total = gain_x[0]
        for xx in range(1, NX):
            total = total + gain_x[xx]
        gain_send[2] = total
        gain_y[y] = total
        for other in (4, 3, 5, 2, 6, 1, 7):
            yy = lax.rem(y + other, NY)
            for cc in range(NC):
                remote(
                    gain_send.at[2], gain_y.at[y], gy_send.at[2 * other + cc], gy_recv.at[y], at(x, z * NC + cc, yy)
                ).start()
        remote(gain_send.at[2], gain_y.at[y], gy_send.at[0], gy_recv.at[y], at(x, z * NC)).start()

    @pl.when(hosted <= DEPTH)
    def _():
        size = jnp.int32(NQ)
        for level in range(1, 4):
            size = jnp.where(hosted == level, 2**level, size)
        mine = jnp.where(hosted < 5, size // 2, 0)

        def add(n, total):
            remote(own, z_recv.at[n], s_send, r_recv.at[n], at(x, q)).wait_recv()
            return total + z_recv[n].astype(F32)

        total = lax.fori_loop(0, mine, add, part[hosted])
        total = lax.fori_loop(mine + 1, size, add, total)
        dkv_buf[0, 1] = key_gradient(own[0], total[0], pl.multiple_of(place[1], T))
        dkv_buf[1, 1] = total[1].astype(BF)

    @pl.when(hosted > DEPTH)
    def _():
        dkv_buf[0, 1] = jnp.zeros((T, D), BF)
        dkv_buf[1, 1] = jnp.zeros((T, D), BF)

    stores.append(pltpu.make_async_copy(dkv_buf.at[0], dk_out, store_sem.at[1]))
    stores.append(pltpu.make_async_copy(dkv_buf.at[1], dv_out, store_sem.at[2]))
    stores[1].start()
    stores[2].start()

    for yy in range(NY):

        @pl.when(jnp.logical_or(c == 0, y != yy))
        def _(yy=yy):
            remote(gain_send.at[2], gain_y.at[yy], gy_send.at[0], gy_recv.at[yy], at(x, q)).wait_recv()

    total = gain_y[0]
    for yy in range(1, NY):
        total = total + gain_y[yy]
    gain_total[...] = total
    stores.append(pltpu.make_async_copy(gain_total.at[pl.ds(0, 1)], dqg_out, store_sem.at[3]))
    stores.append(pltpu.make_async_copy(gain_total.at[pl.ds(1, 1)], dkg_out, store_sem.at[4]))
    stores[3].start()
    stores[4].start()

    def sent(src, sem):
        remote(src, src, sem, sem, at(x, q)).wait_send()

    @pl.when(hosted == 6)
    def _():
        for n in range(NX):
            sent(own, b_send.at[n])

    @pl.when(hosted == 5)
    def _():
        for n in range(2):
            sent(own, b_send.at[n])

    for level in range(1, 5):

        @pl.when(hosted == level)
        def _(level=level):
            for n in range(2**level - 1):
                sent(own, b_send.at[n])

    @pl.when(is_relay)
    def _():
        for n in range(1, 31):
            sent(own, b_send.at[n])

    @pl.when(x != 2)
    def _():
        sent(own, x_sem.at[0])

    @pl.when(lax.rem(x, 2) == 0)
    def _():
        sent(own, x_sem.at[1])

    for zz in range(NZ):

        @pl.when(q != 2 * zz + 1)
        def _(zz=zz):
            sent(gain_send.at[0], gz_send.at[zz])

    for level in range(1, 5):

        @pl.when(q != holder[level])
        def _(level=level):
            sent(own, r_send.at[level])

    @pl.when(jnp.logical_and(x > 0, q != 0))
    def _():
        sent(own, s_send)

    @pl.when(c == 1)
    def _():
        for other in range(1, NX):
            sent(gain_send.at[0], gx_send.at[other])
        for n in range(2, 2 * NY):
            sent(gain_send.at[0], gy_send.at[n])
        sent(gain_send.at[0], gy_send.at[0])

    for store in stores:
        store.wait()


def on_device(queries, keys, values, output_gradient, q_gain, k_gain, leaf_len):
    dma = pltpu.SemaphoreType.DMA
    anywhere = pl.BlockSpec(memory_space=pl.ANY)
    dq, dk, dv, dq_gain, dk_gain = pl.pallas_call(
        kernel,
        name="tree_backward",
        out_shape=[
            jax.ShapeDtypeStruct(queries.shape, BF),
            jax.ShapeDtypeStruct(keys.shape, BF),
            jax.ShapeDtypeStruct(values.shape, BF),
            jax.ShapeDtypeStruct((1, D), F32),
            jax.ShapeDtypeStruct((1, D), F32),
        ],
        in_specs=[anywhere] * 8,
        out_specs=[anywhere] * 5,
        scratch_shapes=[
            pltpu.VMEM((2, T, G * D), BF),
            pltpu.VMEM((2, T, G * D), BF),
            pltpu.VMEM((2, T, D), BF),
            pltpu.VMEM((SLOTS, 2, T, D), BF),
            pltpu.VMEM((1, D), F32),
            pltpu.VMEM((1, D), F32),
            pltpu.SMEM((1,), jnp.int32),
            pltpu.VMEM((KEYS, D), F32),
            pltpu.VMEM((2 * ROWS, D), BF),
            pltpu.VMEM((2 * ROWS, D), F32),
            pltpu.VMEM((2 * ROWS, D), BF),
            pltpu.VMEM((KEYS, D), BF),
            pltpu.VMEM((KEYS, D), F32),
            pltpu.VMEM((KEYS, D), BF),
            pltpu.VMEM((SLOTS, 2, T, D), F32),
            pltpu.VMEM((2 * ROWS, D), F32),
            pltpu.VMEM((2, T, G * D), BF),
            pltpu.VMEM((2, 2, T, D), BF),
            pltpu.VMEM((DEPTH, 2, T, D), BF),
            pltpu.VMEM((2, T, D), BF),
            pltpu.VMEM((4, 2, T, D), BF),
            pltpu.VMEM((NQ, 2, T, D), BF),
            pltpu.VMEM((3, 8, D), F32),
            pltpu.VMEM((NQ, 8, D), F32),
            pltpu.VMEM((NX, 8, D), F32),
            pltpu.VMEM((NY, 8, D), F32),
            pltpu.VMEM((8, D), F32),
            dma((12,)),
            dma((5,)),
            dma((31,)),
            dma((SLOTS,)),
            dma((5,)),
            dma((NQ,)),
            dma((2,)),
            dma((4,)),
            dma(()),
            dma((NZ,)),
            dma((NQ,)),
            dma((NX,)),
            dma((NX,)),
            dma((2 * NY,)),
            dma((NY,)),
        ],
        compiler_params=pltpu.CompilerParams(
            collective_id=0, has_side_effects=True, vmem_limit_bytes=40 * 2**20
        ),
        cost_estimate=pl.CostEstimate(flops=10 * 2 * ROWS * KEYS * D, bytes_accessed=2**20, transcendentals=2 * ROWS * KEYS),
    )(
        queries,
        keys,
        values,
        output_gradient,
        q_gain.reshape(1, D),
        k_gain.reshape(1, D),
        leaf_len,
        jnp.asarray(rope_table()),
    )
    return dq, dk, dv, dq_gain.reshape(D), dk_gain.reshape(D)


def solution(mesh):
    shape = dict(mesh.shape)
    if shape != {"leaf": NX * NZ * NC, "head": NY}:
        raise ValueError("another mesh")
    split = P(None, "leaf", "head")
    return jax.shard_map(
        on_device,
        mesh=mesh,
        in_specs=(split, split, split, split, P(), P(), P("leaf")),
        out_specs=(split, split, split, P(), P()),
        check_vma=False,
    )
```

time: 357 us -> 46.8 us (0.13)
  waiting for transfers between devices: 166 us -> 0 us
  blocking collectives: 99.6 us -> 0 us
  Pallas kernels: 0 us -> 37.2 us
  starting transfers between devices: 35.9 us -> 0 us
  between operations: 15.9 us -> 1.31 us
  other arithmetic: 12.7 us -> 0 us
  matrix products: 8.95 us -> 0 us
  local copies, waits for them, and re-layouts: 16.5 us -> 7.96 us
    all_gather x2 -> x0, waiting for transfers between devices: 163 us -> none  [the longest x1 81.5 us: on_device(): lax.all_gather(host_keys[None], 'leaf', axis=0, tiled=True)]
    psum x1 -> x0, blocking collectives: 99.6 us -> none  [on_device(): dq_gain, dk_gain = lax.psum((dq_part, dk_part), ('leaf', 'head'))]
    pallas_call x0 -> x1, Pallas kernels: none -> 37.2 us  [on_device(): pl.pallas_call(kernel, name='tree_backward', out_shape=[jax.ShapeDtypeStr...]
    ppermute x12 -> x0, starting transfers between devices: 35.9 us -> none  [partner(): lax.ppermute(x, axis, [(i, i ^ 1 << apart) for i in range(lax.axis_size(a...]
    dot_general x35 -> x0, matrix products: 8.95 us -> none  [the longest x7 2.34 us: on_device(): jnp.einsum('kgrs,rkgd->skd', probs_low[slot], output_gradient_rows, prefe...]
    gather x2 -> x0, local copies, waits for them, and re-layouts: 3.57 us -> none  [the longest x1 1.79 us: on_device(): chain_k = jnp.take(every_k, owners, axis=0)]
    unnamed x63 -> x19, local copies, waits for them, and re-layouts: 8.71 us -> 7.96 us
  transfers between devices with their start and end apart: 14 -> 0, of which waited for: 5 -> 0; matrix products, arithmetic and copies ran while one was open for 5% -> 0% of each run, Pallas kernels for 0% -> 0%
where the time goes in v1:
time: 46.8 us; the launch traced here: 46.4 us
  Pallas kernels  37.2 us (79%)
  local copies, waits for them, and re-layouts  7.96 us (17%)
  between operations  1.31 us (3%)
    pallas_call x1, Pallas kernels, on_device(): pl.pallas_call(kernel, name='tree_backward', out_shape=[jax.ShapeDtypeStr...  37.2 us
    unnamed x19, local copies, waits for them, and re-layouts  7.96 us

profile of v1, /device:TPU:1, one launch (start us, length us, event | category | flops | bytes accessed | tf_op | source)
XLA Modules:
  0.0 46.4 jit_solution(16814402892090696026)
XLA Ops:
  1.3 0.0 copy-start.4
  1.3 0.0 copy-start.5
  1.3 0.6 %copy-done.4 = f32[128]{0:T(128)S(1)} copy-done((f32[128]{0:T(128)S(1)}, f32[128]{0:T(128)}, u32[]{:S(2)}) %copy-start.4) | copy-done | bytes 536
  1.9 0.0 copy-done.5
  2.0 0.0 copy-start
  2.0 0.9 %copy-done = bf16[2,64,1024]{2,1,0:T(8,128)(2,1)S(1)} copy-done((bf16[2,64,1024]{2,1,0:T(8,128)(2,1)S(1)}, bf16[2,64,1024]{2,1,0:T(8,128)(2,1)}, u32[]{:S(2)}) %copy-start) | copy-done | bytes 262168
  2.9 0.0 copy-start.1
  2.9 0.9 %copy-done.1 = bf16[2,64,1024]{2,1,0:T(8,128)(2,1)S(1)} copy-done((bf16[2,64,1024]{2,1,0:T(8,128)(2,1)S(1)}, bf16[2,64,1024]{2,1,0:T(8,128)(2,1)}, u32[]{:S(2)}) %copy-start.1) | copy-done | bytes 262168
  3.9 0.0 copy-start.2
  3.9 0.8 %copy-done.2 = bf16[2,64,128]{2,1,0:T(8,128)(2,1)S(1)} copy-done((bf16[2,64,128]{2,1,0:T(8,128)(2,1)S(1)}, bf16[2,64,128]{2,1,0:T(8,128)(2,1)}, u32[]{:S(2)}) %copy-start.2) | copy-done | bytes 32792
  4.6 0.0 copy-start.3
  4.6 0.8 %copy-done.3 = bf16[2,64,128]{2,1,0:T(8,128)(2,1)S(1)} copy-done((bf16[2,64,128]{2,1,0:T(8,128)(2,1)S(1)}, bf16[2,64,128]{2,1,0:T(8,128)(2,1)}, u32[]{:S(2)}) %copy-start.3) | copy-done | bytes 32792
  5.4 0.0 copy-start.6
  5.4 0.9 %copy-done.6 = f32[448,128]{1,0:T(8,128)S(1)} copy-done((f32[448,128]{1,0:T(8,128)S(1)}, f32[448,128]{1,0:T(8,128)}, u32[]{:S(2)}) %copy-start.6) | copy-done | bytes 229400
  6.3 37.2 %tree_backward.1 = (bf16[2,64,1024]{2,1,0:T(8,128)(2,1)S(1)}, bf16[2,64,128]{2,1,0:T(8,128)(2,1)S(1)}, bf16[2,64,128]{2,1,0:T(8,128)(2,1)S(1)}, f32[1,128]{1,0:T(1,128)S(1)}, f32[1,128]{1,0:T(1,128)S(1)}) custom-call(bf16[2,64,1024]{2,1,0:T(8,128)(2,1)S(1)} %copy-done, bf16[2,64,128]{2,1,0:T(8,128)(2,1)S(1)} %copy-done.2, bf16[2,64,128]{2,1,0:T(8,128)(2,1)S(1)} %copy-done.3, ...), custom_call_target="tpu_custom_call" | custom-call | flops 587202560 | bytes 1048576 | tf_op jit(solution)/shard_map/tree_backward/pallas_call | solution.py:507
  43.5 0.7 %copy.19 = bf16[2,64,1024]{2,1,0:T(8,128)(2,1)} copy(bf16[2,64,1024]{2,1,0:T(8,128)(2,1)S(1)} %get-tuple-element.20) | data formatting | bytes 524288
  44.2 0.6 %copy.20 = bf16[2,64,128]{2,1,0:T(8,128)(2,1)} copy(bf16[2,64,128]{2,1,0:T(8,128)(2,1)S(1)} %get-tuple-element.21) | data formatting | bytes 65536
  44.8 0.6 %copy.21 = bf16[2,64,128]{2,1,0:T(8,128)(2,1)} copy(bf16[2,64,128]{2,1,0:T(8,128)(2,1)S(1)} %get-tuple-element.22) | data formatting | bytes 65536
  45.4 0.5 %copy.22 = f32[128]{0:T(128)} copy(f32[128]{0:T(128)S(1)} %bitcast.7) | data formatting | bytes 1024
  45.9 0.5 %copy.23 = f32[128]{0:T(128)} copy(f32[128]{0:T(128)S(1)} %bitcast.6) | data formatting | bytes 1024
Async XLA Ops:
  1.3 0.7 %copy-start.4 = (f32[128]{0:T(128)S(1)}, f32[128]{0:T(128)}, u32[]{:S(2)}) copy-start(f32[128]{0:T(128)} %param.12) | copy-start | bytes 1540
  1.3 0.7 %copy-start.5 = (f32[128]{0:T(128)S(1)}, f32[128]{0:T(128)}, u32[]{:S(2)}) copy-start(f32[128]{0:T(128)} %param.13) | copy-start | bytes 1540
  2.0 0.9 %copy-start = (bf16[2,64,1024]{2,1,0:T(8,128)(2,1)S(1)}, bf16[2,64,1024]{2,1,0:T(8,128)(2,1)}, u32[]{:S(2)}) copy-start(bf16[2,64,1024]{2,1,0:T(8,128)(2,1)} %q_in.1) | copy-start | bytes 786436
  2.9 0.9 %copy-start.1 = (bf16[2,64,1024]{2,1,0:T(8,128)(2,1)S(1)}, bf16[2,64,1024]{2,1,0:T(8,128)(2,1)}, u32[]{:S(2)}) copy-start(bf16[2,64,1024]{2,1,0:T(8,128)(2,1)} %g_in.1) | copy-start | bytes 786436
  3.9 0.8 %copy-start.2 = (bf16[2,64,128]{2,1,0:T(8,128)(2,1)S(1)}, bf16[2,64,128]{2,1,0:T(8,128)(2,1)}, u32[]{:S(2)}) copy-start(bf16[2,64,128]{2,1,0:T(8,128)(2,1)} %k_in.1) | copy-start | bytes 98308
  4.6 0.8 %copy-start.3 = (bf16[2,64,128]{2,1,0:T(8,128)(2,1)S(1)}, bf16[2,64,128]{2,1,0:T(8,128)(2,1)}, u32[]{:S(2)}) copy-start(bf16[2,64,128]{2,1,0:T(8,128)(2,1)} %v_in.1) | copy-start | bytes 98308
  5.4 0.9 %copy-start.6 = (f32[448,128]{1,0:T(8,128)S(1)}, f32[448,128]{1,0:T(8,128)}, u32[]{:S(2)}) copy-start(f32[448,128]{1,0:T(8,128)} %constant.2.clone.table_in) | copy-start | bytes 688132

commit v2 on v1

--- a/solution.py
+++ b/solution.py
@@ -22,6 +22,10 @@
 BF = jnp.bfloat16
 F32 = jnp.float32
 MESH = pl.DeviceIdType.MESH
+AWAY = sorted(
+    ((dx, dy) for dx in range(NX) for dy in range(NY) if dx or dy),
+    key=lambda step: -min(step[0], NX - step[0]) - min(step[1], NY - step[1]),
+)
 
 
 def rope_table():
@@ -55,13 +59,13 @@
 
 
 def kernel(
-    q_in, k_in, v_in, g_in, qg_in, kg_in, len_in, table_in,
+    q_in, k_in, v_in, g_in, qg_in, kg_in, table_in, length,
     dq_out, dk_out, dv_out, dqg_out, dkg_out,
-    q_raw, g_raw, own, kv, qg, kg, length, table,
+    q_raw, g_raw, own, kv, qg, kg, table,
     q_rot, q_unit, g_rows, k_rot, k_unit, v_all, part, y_q, dq_buf, dkv_buf,
-    send_kv, send_sum, x_recv, z_recv, gain_send, gain_z, gain_x, gain_y, gain_total,
+    send_kv, send_sum, x_recv, z_recv, gain_send, gain_z, gain_p, gain_total,
     load_sem, store_sem, b_send, b_recv, r_send, r_recv, x_sem, xr_sem, s_send,
-    gz_send, gz_recv, gx_send, gx_recv, gy_send, gy_recv,
+    gz_send, gz_recv, gp_send, gp_recv, gt_send, gt_recv,
 ):
     leaf = lax.axis_index("leaf")
     y = lax.axis_index("head")
@@ -84,6 +88,7 @@
 
     holder = {level: q // 2**level * 2**level + 2 ** (level - 1) for level in range(1, 5)}
     is_relay = q == 1
+    plane = x * NY + y
     far_owner = jnp.logical_and(q == 0, x > 0)
 
     loads = [
@@ -96,7 +101,6 @@
         pltpu.make_async_copy(kg_in, kg, load_sem.at[6]),
         pltpu.make_async_copy(q_in, q_raw, load_sem.at[7]),
         pltpu.make_async_copy(g_in, g_raw, load_sem.at[8]),
-        pltpu.make_async_copy(len_in, length, load_sem.at[9]),
     ]
     for load in loads:
         load.start()
@@ -124,12 +128,18 @@
         def _(level=level):
             greet(at(x, holder[level]))
 
-    for other in range(1, NY):
-        greet(at(x, z * NC + 1, lax.rem(y + other, NY)))
+    @pl.when(is_relay)
+    def _():
+        def greet_plane(n, carry):
+            there = lax.rem(plane + n, NX * NY)
+            greet(at(there // NY, 1, lax.rem(there, NY)))
+            return carry
+
+        lax.fori_loop(1, NX * NY, greet_plane, 0)
 
     early = jnp.int32(NX - 1)
-    early = early + jnp.where(c == 1, 1 + (NY - 1) * NC, 0)
-    early = early + jnp.where(is_relay, NQ - 1, 0)
+    early = early + jnp.where(c == 1, 1, 0)
+    early = early + jnp.where(is_relay, NQ - 1 + NX * NY - 1, 0)
     for level in (2, 3, 4):
         early = early + jnp.where(hosted == level, 2**level - 1, 0)
     early = early + jnp.where(hosted == 5, 2, 0) + jnp.where(hosted == 6, NX, 0)
@@ -180,9 +190,10 @@
     for load in loads[4:]:
         load.wait()
     q_gain, k_gain = qg[...], kg[...]
+    leaf_len = length[0]
     place = [DEPTH * T, jnp.maximum(DEPTH - hosted, 0) * T]
     live = [
-        lax.broadcasted_iota(jnp.int32, (T, D), 0) < length[0],
+        lax.broadcasted_iota(jnp.int32, (T, D), 0) < leaf_len,
         jnp.broadcast_to(hosted <= DEPTH, (T, D)),
     ]
     for kind in range(2):
@@ -243,7 +254,7 @@
             if kind == 0:
                 piece = scores[slot * T : (slot + 1) * T]
                 if slot == 0:
-                    seen = jnp.logical_and(ahead <= 0, key_at < length[0])
+                    seen = jnp.logical_and(ahead <= 0, key_at < leaf_len)
                     piece = jnp.where(seen, piece, NEG_BIG)
             elif slot == 0:
                 continue
@@ -300,16 +311,12 @@
         cosine, sine = spread(table[(DEPTH - slot) * T : (DEPTH - slot + 1) * T, :])
         back = unturn(part[slot, 0], cosine, sine)
         gain_k = gain_k + jnp.sum(back * k_unit[slot * T : (slot + 1) * T, :], axis=0, keepdims=True)
-    row = lax.broadcasted_iota(jnp.int32, (8, D), 0)
-    terms = jnp.where(row == 0, gain_q, jnp.where(row == 1, gain_k, 0.0))
+    terms = jnp.concatenate([gain_q, gain_k], axis=0)
     gain_send[0] = terms
 
-    for zz in range(NZ):
-        qq = 2 * zz + 1
-
-        @pl.when(q != qq)
-        def _(zz=zz, qq=qq):
-            remote(gain_send.at[0], gain_z.at[q], gz_send.at[zz], gz_recv.at[q], at(x, qq)).start()
+    @pl.when(jnp.logical_not(is_relay))
+    def _():
+        remote(gain_send.at[0], gain_z.at[q], gz_send, gz_recv.at[q], at(x, 1)).start()
 
     for level in range(1, 5):
 
@@ -363,41 +370,33 @@
     def _():
         remote(send_sum, z_recv.at[q], s_send, r_recv.at[q], at(x, 0)).start()
 
-    @pl.when(c == 1)
-    def _():
-        gain_z[q] = terms
-        for zz in range(NZ):
-            for cc in range(NC):
-                qq = zz * NC + cc
-
-                @pl.when(q != qq)
-                def _(qq=qq):
-                    remote(gain_send.at[0], gain_z.at[qq], gz_send.at[0], gz_recv.at[qq], at(x, qq)).wait_recv()
-
-        total = gain_z[0]
+    @pl.when(is_relay)
+    def _():
+        gain_z[1] = terms
+        for qq in range(NQ):
+            if qq != 1:
+                remote(gain_send.at[0], gain_z.at[qq], gz_send, gz_recv.at[qq], at(x, qq)).wait_recv()
+        line = gain_z[0]
         for qq in range(1, NQ):
-            total = total + gain_z[qq]
-        gain_send[1] = total
-        gain_x[x] = total
-        for other in range(1, NX):
-            remote(
-                gain_send.at[1], gain_x.at[x], gx_send.at[other], gx_recv.at[x], at(lax.rem(x + other, NX), q)
-            ).start()
-        for other in range(1, NX):
-            xx = lax.rem(x + other, NX)
-            remote(gain_send.at[1], gain_x.at[xx], gx_send.at[other], gx_recv.at[xx], at(xx, q)).wait_recv()
-        total = gain_x[0]
-        for xx in range(1, NX):
-            total = total + gain_x[xx]
-        gain_send[2] = total
-        gain_y[y] = total
-        for other in (4, 3, 5, 2, 6, 1, 7):
-            yy = lax.rem(y + other, NY)
-            for cc in range(NC):
-                remote(
-                    gain_send.at[2], gain_y.at[y], gy_send.at[2 * other + cc], gy_recv.at[y], at(x, z * NC + cc, yy)
-                ).start()
-        remote(gain_send.at[2], gain_y.at[y], gy_send.at[0], gy_recv.at[y], at(x, z * NC)).start()
+            line = line + gain_z[qq]
+        gain_send[1] = line
+        gain_p[plane] = line
+        for n, (dx, dy) in enumerate(AWAY):
+            device = at(lax.rem(x + dx, NX), 1, lax.rem(y + dy, NY))
+            remote(gain_send.at[1], gain_p.at[plane], gp_send.at[n], gp_recv.at[plane], device).start()
+
+        def arrived(n, carry):
+            there = lax.rem(plane + n, NX * NY)
+            remote(gain_send.at[1], gain_p.at[there], gp_send.at[0], gp_recv.at[there], at(x, 1)).wait_recv()
+            return carry
+
+        lax.fori_loop(1, NX * NY, arrived, 0)
+        total = gain_p[0]
+        for n in range(1, NX * NY):
+            total = total + gain_p[n]
+        gain_total[...] = total
+        for n, qq in enumerate(others):
+            remote(gain_total, gain_total, gt_send.at[n], gt_recv, at(x, qq)).start()
 
     @pl.when(hosted <= DEPTH)
     def _():
@@ -425,16 +424,10 @@
     stores[1].start()
     stores[2].start()
 
-    for yy in range(NY):
-
-        @pl.when(jnp.logical_or(c == 0, y != yy))
-        def _(yy=yy):
-            remote(gain_send.at[2], gain_y.at[yy], gy_send.at[0], gy_recv.at[yy], at(x, q)).wait_recv()
-
-    total = gain_y[0]
-    for yy in range(1, NY):
-        total = total + gain_y[yy]
-    gain_total[...] = total
+    @pl.when(jnp.logical_not(is_relay))
+    def _():
+        remote(gain_total, gain_total, gz_send, gt_recv, at(x, 1)).wait_recv()
+
     stores.append(pltpu.make_async_copy(gain_total.at[pl.ds(0, 1)], dqg_out, store_sem.at[3]))
     stores.append(pltpu.make_async_copy(gain_total.at[pl.ds(1, 1)], dkg_out, store_sem.at[4]))
     stores[3].start()
@@ -473,11 +466,9 @@
     def _():
         sent(own, x_sem.at[1])
 
-    for zz in range(NZ):
-
-        @pl.when(q != 2 * zz + 1)
-        def _(zz=zz):
-            sent(gain_send.at[0], gz_send.at[zz])
+    @pl.when(jnp.logical_not(is_relay))
+    def _():
+        sent(gain_total, gz_send)
 
     for level in range(1, 5):
 
@@ -489,32 +480,40 @@
     def _():
         sent(own, s_send)
 
-    @pl.when(c == 1)
-    def _():
-        for other in range(1, NX):
-            sent(gain_send.at[0], gx_send.at[other])
-        for n in range(2, 2 * NY):
-            sent(gain_send.at[0], gy_send.at[n])
-        sent(gain_send.at[0], gy_send.at[0])
+    @pl.when(is_relay)
+    def _():
+        for n in range(len(AWAY)):
+            sent(gain_total, gp_send.at[n])
+        for n in range(len(others)):
+            sent(gain_total, gt_send.at[n])
 
     for store in stores:
         store.wait()
+
+
+def hand_over(*refs):
+    copies = [pltpu.make_async_copy(refs[n], refs[5 + n], refs[10].at[n]) for n in range(5)]
+    for copy in copies:
+        copy.start()
+    for copy in copies:
+        copy.wait()
 
 
 def on_device(queries, keys, values, output_gradient, q_gain, k_gain, leaf_len):
     dma = pltpu.SemaphoreType.DMA
     anywhere = pl.BlockSpec(memory_space=pl.ANY)
-    dq, dk, dv, dq_gain, dk_gain = pl.pallas_call(
+    in_hbm = pl.BlockSpec(memory_space=pltpu.HBM)
+    results = pl.pallas_call(
         kernel,
         name="tree_backward",
         out_shape=[
-            jax.ShapeDtypeStruct(queries.shape, BF),
-            jax.ShapeDtypeStruct(keys.shape, BF),
-            jax.ShapeDtypeStruct(values.shape, BF),
-            jax.ShapeDtypeStruct((1, D), F32),
-            jax.ShapeDtypeStruct((1, D), F32),
+            pltpu.VMEM(queries.shape, BF),
+            pltpu.VMEM(keys.shape, BF),
+            pltpu.VMEM(values.shape, BF),
+            pltpu.VMEM((1, D), F32),
+            pltpu.VMEM((1, D), F32),
         ],
-        in_specs=[anywhere] * 8,
+        in_specs=[anywhere] * 7 + [pl.BlockSpec(memory_space=pltpu.SMEM)],
         out_specs=[anywhere] * 5,
         scratch_shapes=[
             pltpu.VMEM((2, T, G * D), BF),
@@ -523,7 +522,6 @@
             pltpu.VMEM((SLOTS, 2, T, D), BF),
             pltpu.VMEM((1, D), F32),
             pltpu.VMEM((1, D), F32),
-            pltpu.SMEM((1,), jnp.int32),
             pltpu.VMEM((KEYS, D), F32),
             pltpu.VMEM((2 * ROWS, D), BF),
             pltpu.VMEM((2 * ROWS, D), F32),
@@ -539,11 +537,10 @@
             pltpu.VMEM((2, T, D), BF),
             pltpu.VMEM((4, 2, T, D), BF),
             pltpu.VMEM((NQ, 2, T, D), BF),
-            pltpu.VMEM((3, 8, D), F32),
-            pltpu.VMEM((NQ, 8, D), F32),
-            pltpu.VMEM((NX, 8, D), F32),
-            pltpu.VMEM((NY, 8, D), F32),
-            pltpu.VMEM((8, D), F32),
+            pltpu.VMEM((2, 2, D), F32),
+            pltpu.VMEM((NQ, 2, D), F32),
+            pltpu.VMEM((NX * NY, 2, D), F32),
+            pltpu.VMEM((2, D), F32),
             dma((12,)),
             dma((5,)),
             dma((31,)),
@@ -553,27 +550,41 @@
             dma((2,)),
             dma((4,)),
             dma(()),
-            dma((NZ,)),
+            dma(()),
             dma((NQ,)),
-            dma((NX,)),
-            dma((NX,)),
-            dma((2 * NY,)),
-            dma((NY,)),
+            dma((NX * NY - 1,)),
+            dma((NX * NY,)),
+            dma((NQ - 1,)),
+            dma(()),
         ],
         compiler_params=pltpu.CompilerParams(
             collective_id=0, has_side_effects=True, vmem_limit_bytes=40 * 2**20
         ),
         cost_estimate=pl.CostEstimate(flops=10 * 2 * ROWS * KEYS * D, bytes_accessed=2**20, transcendentals=2 * ROWS * KEYS),
     )(
-        queries,
-        keys,
-        values,
-        output_gradient,
-        q_gain.reshape(1, D),
-        k_gain.reshape(1, D),
+        *(
+            pltpu.with_memory_space_constraint(array, pltpu.HBM)
+            for array in (
+                queries,
+                keys,
+                values,
+                output_gradient,
+                q_gain.reshape(1, D),
+                k_gain.reshape(1, D),
+                jnp.asarray(rope_table()),
+            )
+        ),
         leaf_len,
-        jnp.asarray(rope_table()),
     )
+    dq, dk, dv, dq_gain, dk_gain = pl.pallas_call(
+        hand_over,
+        name="hand_over",
+        out_shape=[jax.ShapeDtypeStruct(r.shape, r.dtype) for r in results],
+        in_specs=[anywhere] * 5,
+        out_specs=[in_hbm] * 5,
+        scratch_shapes=[dma((5,))],
+        compiler_params=pltpu.CompilerParams(vmem_limit_bytes=8 * 2**20),
+    )(*(pltpu.with_memory_space_constraint(r, pltpu.VMEM) for r in results))
     return dq, dk, dv, dq_gain.reshape(D), dk_gain.reshape(D)
 
 

time: 46.8 us -> 38.4 us (0.82)
  local copies, waits for them, and re-layouts: 7.96 us -> 0 us
    unnamed x19 -> x0, local copies, waits for them, and re-layouts: 7.96 us -> none
    pallas_call x1 -> x2, Pallas kernels: 37.2 us -> 36.9 us  [the longest x1 36.2 us: on_device(): pl.pallas_call(kernel, name='tree_backward', out_shape=[pltpu.VMEM(querie...]
where the time goes in v2:
time: 38.4 us; the launch traced here: 38.2 us
  Pallas kernels  36.9 us (96%)
  between operations  1.29 us (3%)
    pallas_call x1, Pallas kernels, on_device(): pl.pallas_call(kernel, name='tree_backward', out_shape=[pltpu.VMEM(querie...  36.2 us

profile of v2, /device:TPU:1, one launch (start us, length us, event | category | flops | bytes accessed | tf_op | source)
XLA Modules:
  0.0 38.2 jit_solution(6963615550705435161)
XLA Ops:
  1.3 36.2 %tree_backward.1 = (bf16[2,64,1024]{2,1,0:T(8,128)(2,1)S(1)}, bf16[2,64,128]{2,1,0:T(8,128)(2,1)S(1)}, bf16[2,64,128]{2,1,0:T(8,128)(2,1)S(1)}, f32[1,128]{1,0:T(1,128)S(1)}, f32[1,128]{1,0:T(1,128)S(1)}) custom-call(bf16[2,64,1024]{2,1,0:T(8,128)(2,1)} %q_in.1, bf16[2,64,128]{2,1,0:T(8,128)(2,1)} %k_in.1, bf16[2,64,128]{2,1,0:T(8,128)(2,1)} %v_in.1, ...), custom_call_target="tpu_custom_call" | custom-call | flops 587202560 | bytes 1048576 | tf_op jit(solution)/shard_map/tree_backward/pallas_call | solution.py:506
  37.5 0.8 %hand_over.1 = (bf16[2,64,1024]{2,1,0:T(8,128)(2,1)}, bf16[2,64,128]{2,1,0:T(8,128)(2,1)}, bf16[2,64,128]{2,1,0:T(8,128)(2,1)}, f32[1,128]{1,0:T(1,128)}, f32[1,128]{1,0:T(1,128)}) custom-call(bf16[2,64,1024]{2,1,0:T(8,128)(2,1)S(1)} %get-tuple-element.15.refs_0_, bf16[2,64,128]{2,1,0:T(8,128)(2,1)S(1)} %get-tuple-element.16.refs_1_, ...), custom_call_target="tpu_custom_call" | custom-call | tf_op jit(solution)/shard_map/hand_over/pallas_call | solution.py:579

commit v3 on v2

v3 whole, which is shorter than its diff:
```python
import jax
import jax.numpy as jnp
import numpy as np
from jax import lax
from jax.experimental import pallas as pl
from jax.experimental.pallas import tpu as pltpu
from jax.sharding import PartitionSpec as P

NEG_BIG = -1000000000.0
NORM_EPS = 1e-06
ROPE_BASE = 1000000.0
DEPTH = 6
T = 64
D = 128
G = 8
SLOTS = DEPTH + 1
KEYS = SLOTS * T
NEAR = 4
ROWS = G * T
NX, NZ, NC, NY = 4, 8, 2, 8
NQ = NZ * NC
SCALE = D ** (-0.5)
BF = jnp.bfloat16
F32 = jnp.float32
MESH = pl.DeviceIdType.MESH
SERVED = ((1, (13, 15, 3)), (5, (11, 9, 7)))
AWAY = sorted(
    ((dx, dy) for dx in range(NX) for dy in range(NY) if dx or dy),
    key=lambda step: -min(step[0], NX - step[0]) - min(step[1], NY - step[1]),
)


def rope_table():
    frequency = (ROPE_BASE ** (-(np.arange(D // 2, dtype=np.float32) * 2.0 / D))).astype(np.float32)
    angles = np.arange(KEYS, dtype=np.float32)[:, None] * frequency
    return np.concatenate([np.cos(angles), np.sin(angles)], axis=1).astype(np.float32)


def spread(table):
    lane = lax.broadcasted_iota(jnp.int32, table.shape, 1)
    other = pltpu.roll(table, D // 2, axis=1)
    low = lane < D // 2
    return jnp.where(low, table, other), jnp.where(low, -other, table)


def turn(x, cosine, sine):
    return x * cosine + pltpu.roll(x, D // 2, axis=1) * sine


def unturn(x, cosine, sine):
    return x * cosine - pltpu.roll(x, D // 2, axis=1) * sine


def unit_of(x):
    factor = lax.rsqrt(jnp.mean(x * x, axis=-1, keepdims=True) + NORM_EPS)
    return x * factor, factor


def dot(a, b, contract):
    return lax.dot_general(a, b, (contract, ((), ())), preferred_element_type=F32)


def kernel(
    q_in, k_in, v_in, g_in, qg_in, kg_in, table_in, length,
    dq_out, dk_out, dv_out, dqg_out, dkg_out,
    q_raw, g_raw, own, kv, qg, kg, table,
    q_rot, g_rows, k_rot, v_all, wq_cos, wq_sin, wk_cos, wk_sin, near_e, near_d, near_s, probs, dscores, part, y_q, ballast,
    send_kv, send_sum, x_recv, z_recv, gain_send, gain_z, gain_p, gain_total,
    load_sem, b_send, b_recv, r_send, r_recv, x_sem, xr_sem, s_send,
    gz_send, gz_recv, gp_send, gp_recv, gt_send, gt_recv,
):
    leaf = lax.axis_index("leaf")
    y = lax.axis_index("head")
    x = leaf // NQ
    q = lax.rem(leaf, NQ)
    z = q // NC
    c = lax.rem(q, NC)

    def at(xx, qq, yy=None):
        return (xx * NQ + qq, y if yy is None else yy)

    hosted = jnp.int32(1)
    for level in range(1, DEPTH + 1):
        hosted = hosted + jnp.where(lax.rem(leaf, 2**level) == 0, 1, 0)

    def remote(src, dst, send, recv, device):
        return pltpu.make_async_remote_copy(
            src_ref=src, dst_ref=dst, send_sem=send, recv_sem=recv, device_id=device, device_id_type=MESH
        )

    def settle(count, sem):
        blocks = ballast.at[pl.ds(0, count)]
        pltpu.make_async_copy(blocks, blocks, sem).wait()

    holder = {level: q // 2**level * 2**level + 2 ** (level - 1) for level in range(1, 5)}
    is_relay = q == 1
    is_near = q == 5
    is_second = q == 9
    far_owner = jnp.logical_and(q == 0, x > 0)
    plane = x * NY + y

    def among(places):
        here = q == places[0]
        for place in places[1:]:
            here = jnp.logical_or(here, q == place)
        return here

    barrier = pltpu.get_barrier_semaphore()

    def greet(device):
        pl.semaphore_signal(barrier, inc=1, device_id=device, device_id_type=MESH)

    for relay, served in SERVED:

        @pl.when(among(served))
        def _(relay=relay):
            greet(at(x, relay))

    @pl.when(z > 4)
    def _():
        greet(at(x, 9))

    @pl.when(jnp.logical_or(z < 4, is_second))
    def _():
        greet(at(x, 8))

    for level in (3, 2, 1):

        @pl.when(q != holder[level])
        def _(level=level):
            greet(at(x, holder[level]))

    @pl.when(jnp.logical_or(is_relay, is_near))
    def _():
        greet(at(2, 0))
        greet(at(x // 2 * 2 + 1, 0))

    for other in range(1, NX):
        greet(at(lax.rem(x + other, NX), q))

    early = jnp.int32(NX - 1)
    early = early + jnp.where(c == 1, 1, 0)
    early = early + jnp.where(is_relay, 3 + NX * NY - 1, 0) + jnp.where(is_near, 3, 0)
    early = early + jnp.where(is_second, 6, 0)
    for level, count in ((2, 3), (3, 7), (4, 9), (5, 4), (6, 2 * NX)):
        early = early + jnp.where(hosted == level, count, 0)

    loads = [
        pltpu.make_async_copy(k_in.at[1], own.at[0], load_sem.at[0]),
        pltpu.make_async_copy(v_in.at[1], own.at[1], load_sem.at[0]),
        pltpu.make_async_copy(k_in.at[0], kv.at[0, 0], load_sem.at[1]),
        pltpu.make_async_copy(v_in.at[0], kv.at[0, 1], load_sem.at[1]),
        pltpu.make_async_copy(table_in, table, load_sem.at[2]),
        pltpu.make_async_copy(qg_in, qg, load_sem.at[3]),
        pltpu.make_async_copy(kg_in, kg, load_sem.at[4]),
        pltpu.make_async_copy(q_in, q_raw, load_sem.at[5]),
        pltpu.make_async_copy(g_in, g_raw, load_sem.at[6]),
    ]
    for load in loads:
        load.start()

    @pl.when(is_relay)
    def _():
        def greet_plane(n, carry):
            there = lax.rem(plane + n, NX * NY)
            greet(at(there // NY, 1, lax.rem(there, NY)))
            return carry

        lax.fori_loop(1, NX * NY, greet_plane, 0)

    settle(1, load_sem.at[0])

    pl.semaphore_wait(barrier, early)

    @pl.when(jnp.logical_and(far_owner, x == 2))
    def _():
        for relay in (5, 1):
            for xx in range(NX):
                remote(own, kv.at[6], b_send, b_recv.at[6], at(xx, relay)).start()

    @pl.when(jnp.logical_and(far_owner, x != 2))
    def _():
        for relay in (5, 1):
            for n in range(2):
                remote(own, kv.at[5], b_send, b_recv.at[5], at(x - n, relay)).start()

    for level in (4, 3, 2, 1):

        @pl.when(hosted == level)
        def _(level=level):
            half = 2 ** (level - 1)
            offsets = sorted((o for o in range(-half, half) if o), key=lambda o: -abs(o))
            if level == 4:
                offsets = [1] + [o for o in offsets if o < 0]
            for offset in offsets:
                remote(own, kv.at[level], b_send, b_recv.at[level], at(x, q + offset)).start()
            for n in range(2):
                pltpu.make_async_copy((k_in, v_in)[n].at[1], kv.at[level, n], load_sem.at[7]).start()

    @pl.when(is_second)
    def _():
        remote(own, kv.at[4], b_send, b_recv.at[4], at(x, 8)).wait_recv()
        for qq in (15, 14, 13, 12, 11, 10):
            remote(kv.at[4], kv.at[4], b_send, b_recv.at[4], at(x, qq)).start()

    top_two = kv.at[pl.ds(5, 2)]

    for relay, served in SERVED:

        @pl.when(q == relay)
        def _(relay=relay, served=served):
            for level in (5, 6):
                remote(own, kv.at[level], b_send, b_recv.at[level], at(x, 0)).wait_recv()
            for qq in (*served, relay - 1):
                remote(top_two, top_two, b_send, b_recv.at[5], at(x, qq)).start()

    for load in loads[4:]:
        load.wait()
    q_gain, k_gain = qg[...], kg[...]
    leaf_len = length[0]
    place = [DEPTH * T, jnp.maximum(DEPTH - hosted, 0) * T]
    live = [
        lax.broadcasted_iota(jnp.int32, (T, D), 0) < leaf_len,
        jnp.broadcast_to(hosted <= DEPTH, (T, D)),
    ]
    for kind in range(2):
        cosine, sine = spread(table[pl.ds(pl.multiple_of(place[kind], T), T), :])
        w_cos, w_sin = [], []
        for head in range(G):
            rows = pl.ds(kind * ROWS + head * T, T)
            unit, _ = unit_of(q_raw[kind, :, head * D : (head + 1) * D].astype(F32))
            q_rot[rows, :] = turn(unit * q_gain, cosine, sine).astype(BF)
            w_cos.append(unit * cosine)
            w_sin.append(pltpu.roll(unit * sine, D // 2, axis=1))
            if head % 2:
                pair = slice(kind * ROWS + (head - 1) * T, kind * ROWS + (head + 1) * T)
                wq_cos[:, pair] = jnp.transpose(jnp.concatenate(w_cos[-2:], axis=0))
                wq_sin[:, pair] = jnp.transpose(jnp.concatenate(w_sin[-2:], axis=0))
            grad = g_raw[kind, :, head * D : (head + 1) * D]
            g_rows[rows, :] = jnp.where(live[kind], grad, jnp.zeros((), BF))

    settle(1, load_sem.at[1])

    def take(slot):
        rows = pl.ds(slot * T, T)
        cosine, sine = spread(table[(DEPTH - slot) * T : (DEPTH - slot + 1) * T, :])
        unit, _ = unit_of(kv[slot, 0].astype(F32))
        wk_cos[rows, :] = unit * cosine
        wk_sin[rows, :] = pltpu.roll(unit * sine, D // 2, axis=1)
        k_rot[rows, :] = turn(unit * k_gain, cosine, sine).astype(BF)
        v_all[rows, :] = kv[slot, 1]

    def from_holder(level):
        @pl.when(jnp.logical_and(q != holder[level], jnp.logical_not(jnp.logical_and(is_second, level == 4))))
        def _():
            remote(own, kv.at[level], b_send, b_recv.at[level], at(x, holder[level])).wait_recv()

        @pl.when(hosted == level)
        def _():
            settle(1, load_sem.at[7])

    take(0)
    for level in (1, 2, 3):
        from_holder(level)
        take(level)

    key_at = lax.broadcasted_iota(jnp.int32, (T, ROWS), 0)
    row_at = lax.rem(lax.broadcasted_iota(jnp.int32, (T, ROWS), 1), T)
    ahead = key_at - row_at

    def partial(first, last, kind):
        rows = slice(kind * ROWS, (kind + 1) * ROWS)
        slots = slice(first * T, last * T)
        scores = dot(k_rot[slots, :], q_rot[rows, :], ((1,), (1,))) * SCALE
        pieces = []
        for slot in range(first, last):
            piece = scores[(slot - first) * T : (slot - first + 1) * T]
            if kind == 0:
                if slot == 0:
                    seen = jnp.logical_and(ahead <= 0, key_at < leaf_len)
                    piece = jnp.where(seen, piece, NEG_BIG)
            elif slot == 0:
                piece = jnp.full_like(piece, NEG_BIG)
            else:
                bound = jnp.where(hosted == slot, 0, jnp.where(hosted < slot, T, -T))
                piece = jnp.where(ahead <= bound, piece, NEG_BIG)
            pieces.append(piece)
        scores = jnp.concatenate(pieces, axis=0)
        top = jnp.max(scores, axis=0, keepdims=True)
        raised = jnp.exp(scores - top)
        dprobs = dot(v_all[slots, :], g_rows[rows, :], ((1,), (1,)))
        return (
            raised,
            dprobs,
            top,
            jnp.sum(raised, axis=0, keepdims=True),
            jnp.sum(raised * dprobs, axis=0, keepdims=True),
        )

    for kind in range(2):
        rows = slice(kind * ROWS, (kind + 1) * ROWS)
        near_e[:, rows], near_d[:, rows], near_s[0:1, rows], near_s[1:2, rows], near_s[2:3, rows] = partial(0, NEAR, kind)

    @pl.when(jnp.logical_not(jnp.logical_or(is_relay, is_near)))
    def _():
        remote(top_two, top_two, b_send, b_recv.at[5], at(x, 1)).wait_recv()

        @pl.when(c == 1)
        def _():
            remote(top_two, top_two, b_send, b_recv.at[5], at(x, q - 1)).start()

    take(5)
    take(6)
    from_holder(4)
    take(4)

    for kind in range(2):
        rows = slice(kind * ROWS, (kind + 1) * ROWS)
        far_e, far_d, far_top, far_sum, far_delta = partial(NEAR, SLOTS, kind)
        near_top = near_s[0:1, rows]
        top = jnp.maximum(near_top, far_top)
        near_f, far_f = jnp.exp(near_top - top), jnp.exp(far_top - top)
        over = 1.0 / (near_s[1:2, rows] * near_f + far_sum * far_f)
        near_f, far_f = near_f * over, far_f * over
        delta = near_s[2:3, rows] * near_f + far_delta * far_f
        near = near_e[:, rows] * near_f
        far = far_e * far_f
        probs[: NEAR * T, rows] = near.astype(BF)
        probs[NEAR * T :, rows] = far.astype(BF)
        dscores[: NEAR * T, rows] = (near * (near_d[:, rows] - delta)).astype(BF)
        dscores[NEAR * T :, rows] = (far * (far_d - delta)).astype(BF)
    dk_all = dot(dscores[...], q_rot[...], ((1,), (0,))) * SCALE
    dv_all = dot(probs[...], g_rows[...], ((1,), (0,)))
    dq_turned = dot(k_rot[...], dscores[...], ((0,), (0,))) * SCALE
    for slot in range(SLOTS):
        part[slot, 0] = dk_all[slot * T : (slot + 1) * T]
        part[slot, 1] = dv_all[slot * T : (slot + 1) * T]

    for slot in range(1, SLOTS):
        send_kv[slot - 1] = part[slot].astype(BF)

    @pl.when(x != 2)
    def _():
        n = jnp.minimum(x, 2)
        remote(send_kv.at[5], x_recv.at[n], x_sem.at[0], xr_sem, at(2, q)).start()

    @pl.when(lax.rem(x, 2) == 0)
    def _():
        remote(send_kv.at[4], x_recv.at[3], x_sem.at[1], xr_sem, at(x + 1, q)).start()

    straight, crossed = dq_turned * wq_cos[...], dq_turned * wq_sin[...]
    both = straight - jnp.concatenate([crossed[D // 2 :], crossed[: D // 2]], axis=0)
    lanes = both[:, :D]
    for n in range(1, 2 * ROWS // D):
        lanes = lanes + both[:, n * D : (n + 1) * D]
    gain_q = jnp.sum(jnp.transpose(lanes), axis=0, keepdims=True)
    gain_k = jnp.sum(dk_all * wk_cos[...], axis=0, keepdims=True) - pltpu.roll(
        jnp.sum(dk_all * wk_sin[...], axis=0, keepdims=True), D // 2, axis=1
    )
    terms = jnp.concatenate([gain_q, gain_k], axis=0)
    gain_send[0] = terms

    @pl.when(jnp.logical_not(is_relay))
    def _():
        remote(gain_send.at[0], gain_z.at[lax.rem(q + NQ - 2, NQ)], gz_send, gz_recv, at(x, 1)).start()

    for level in range(1, 5):

        @pl.when(q != holder[level])
        def _(level=level):
            n = lax.rem(q, 2**level)
            n = jnp.where(n > 2 ** (level - 1), n - 1, n)
            remote(send_kv.at[level - 1], z_recv.at[n], r_send, r_recv, at(x, holder[level])).start()

    y_q[...] = jnp.transpose(dq_turned)
    for kind in range(2):
        cosine, sine = spread(table[pl.ds(pl.multiple_of(place[kind], T), T), :])
        for head in range(G):
            rows = pl.ds(kind * ROWS + head * T, T)
            columns = slice(head * D, (head + 1) * D)
            raw = q_raw[kind, :, columns].astype(F32)
            unit, factor = unit_of(raw)
            scaled = unturn(y_q[rows, :], cosine, sine) * q_gain
            inner = jnp.mean(scaled * unit, axis=-1, keepdims=True)
            dq_out[kind, :, columns] = (factor * (scaled - unit * inner)).astype(BF)

    def key_gradient(raw, turned, start):
        cosine, sine = spread(table[pl.ds(start, T), :])
        unit, factor = unit_of(raw.astype(F32))
        scaled = unturn(turned, cosine, sine) * k_gain
        inner = jnp.mean(scaled * unit, axis=-1, keepdims=True)
        return (factor * (scaled - unit * inner)).astype(BF)

    dk_out[0] = key_gradient(kv[0, 0], part[0, 0], DEPTH * T)
    dv_out[0] = part[0, 1].astype(BF)

    @pl.when(x == 2)
    def _():
        settle(3, xr_sem)
        total = part[6]
        for n in range(3):
            total = total + x_recv[n].astype(F32)
        part[6] = total
        send_sum[...] = total.astype(BF)

    @pl.when(lax.rem(x, 2) == 1)
    def _():
        settle(1, xr_sem)
        total = part[5] + x_recv[3].astype(F32)
        part[5] = total
        send_sum[...] = total.astype(BF)

    @pl.when(jnp.logical_and(x > 0, q != 0))
    def _():
        remote(send_sum, z_recv.at[q - 1], s_send, r_recv, at(x, 0)).start()

    @pl.when(among((1, 5, 9)))
    def _():
        settle(9, b_send)

    @pl.when(among((3, 7, 11, 13, 15)))
    def _():
        settle(3, b_send)

    for level, count in ((2, 3), (3, 7), (4, 9), (5, 4), (6, 2 * NX)):

        @pl.when(hosted == level)
        def _(count=count):
            settle(count, b_send)

    @pl.when(hosted <= DEPTH)
    def _():
        size = jnp.int32(NQ)
        for level in range(1, 4):
            size = jnp.where(hosted == level, 2**level, size)
        for level in range(1, DEPTH + 1):

            @pl.when(hosted == level)
            def _(level=level):
                settle(2 ** min(level, 4) - 1, r_recv)

        def add(n, total):
            return total + z_recv[n].astype(F32)

        total = lax.fori_loop(0, size - 1, add, part[hosted])
        dk_out[1] = key_gradient(own[0], total[0], pl.multiple_of(place[1], T))
        dv_out[1] = total[1].astype(BF)

    @pl.when(hosted > DEPTH)
    def _():
        dk_out[1] = jnp.zeros((T, D), BF)
        dv_out[1] = jnp.zeros((T, D), BF)

    @pl.when(is_relay)
    def _():
        gain_z[NQ - 1] = terms
        lines = gain_z.at[pl.ds(0, NQ - 1)]
        pltpu.make_async_copy(lines, lines, gz_recv).wait()
        line = gain_z[0]
        for qq in range(1, NQ):
            line = line + gain_z[qq]
        gain_send[1] = line
        gain_p[plane] = line
        for dx, dy in AWAY:
            device = at(lax.rem(x + dx, NX), 1, lax.rem(y + dy, NY))
            remote(gain_send.at[1], gain_p.at[plane], gp_send, gp_recv, device).start()

        away = gain_p.at[pl.ds(0, len(AWAY))]
        pltpu.make_async_copy(away, away, gp_recv).wait()
        total = gain_p[0]
        for n in range(1, NX * NY):
            total = total + gain_p[n]
        gain_total[...] = total
        for qq in (3, 5, 0):
            remote(gain_total, gain_total, gt_send, gt_recv, at(x, qq)).start()
        pltpu.make_async_copy(away, away, gp_send).wait()

    @pl.when(x != 2)
    def _():
        settle(1, x_sem.at[0])

    @pl.when(lax.rem(x, 2) == 0)
    def _():
        settle(1, x_sem.at[1])

    @pl.when(hosted < 5)
    def _():
        settle(3, r_send)

    @pl.when(hosted >= 5)
    def _():
        settle(4, r_send)

    @pl.when(jnp.logical_and(x > 0, q != 0))
    def _():
        settle(1, s_send)

    @pl.when(jnp.logical_not(is_relay))
    def _():
        pltpu.make_async_copy(gain_total, gain_total, gz_send).wait()
        pltpu.make_async_copy(gain_total, gain_total, gt_recv).wait()

    def pass_on(when, targets):
        @pl.when(when)
        def _():
            for qq in targets:
                remote(gain_total, gain_total, gt_send, gt_recv, at(x, qq)).start()

    pass_on(q == 0, (15, 13, 11))
    pass_on(q == 5, (7, 9, 4))
    pass_on(jnp.logical_and(c == 1, jnp.logical_and(q != 5, q != 1)), (q - 1,))
    dqg_out[...] = gain_total[0:1]
    dkg_out[...] = gain_total[1:2]

    def passed(when, count):
        @pl.when(when)
        def _():
            sent = gain_z.at[pl.ds(0, count)]
            pltpu.make_async_copy(sent, sent, gt_send).wait()

    passed(jnp.logical_or(q < 2, q == 5), 3)
    passed(jnp.logical_and(c == 1, jnp.logical_and(q != 5, q != 1)), 1)


def hand_over(*refs):
    copies = [pltpu.make_async_copy(refs[n], refs[5 + n], refs[10].at[n]) for n in range(5)]
    for copy in copies:
        copy.start()
    for copy in copies:
        copy.wait()


def on_device(queries, keys, values, output_gradient, q_gain, k_gain, leaf_len):
    dma = pltpu.SemaphoreType.DMA
    anywhere = pl.BlockSpec(memory_space=pl.ANY)
    in_hbm = pl.BlockSpec(memory_space=pltpu.HBM)
    results = pl.pallas_call(
        kernel,
        name="tree_backward",
        out_shape=[
            pltpu.VMEM(queries.shape, BF),
            pltpu.VMEM(keys.shape, BF),
            pltpu.VMEM(values.shape, BF),
            pltpu.VMEM((1, D), F32),
            pltpu.VMEM((1, D), F32),
        ],
        in_specs=[anywhere] * 7 + [pl.BlockSpec(memory_space=pltpu.SMEM)],
        out_specs=[pl.BlockSpec(memory_space=pltpu.VMEM)] * 5,
        scratch_shapes=[
            pltpu.VMEM((2, T, G * D), BF),
            pltpu.VMEM((2, T, G * D), BF),
            pltpu.VMEM((2, T, D), BF),
            pltpu.VMEM((SLOTS, 2, T, D), BF),
            pltpu.VMEM((1, D), F32),
            pltpu.VMEM((1, D), F32),
            pltpu.VMEM((KEYS, D), F32),
            pltpu.VMEM((2 * ROWS, D), BF),
            pltpu.VMEM((2 * ROWS, D), BF),
            pltpu.VMEM((KEYS, D), BF),
            pltpu.VMEM((KEYS, D), BF),
            pltpu.VMEM((D, 2 * ROWS), F32),
            pltpu.VMEM((D, 2 * ROWS), F32),
            pltpu.VMEM((KEYS, D), F32),
            pltpu.VMEM((KEYS, D), F32),
            pltpu.VMEM((NEAR * T, 2 * ROWS), F32),
            pltpu.VMEM((NEAR * T, 2 * ROWS), F32),
            pltpu.VMEM((8, 2 * ROWS), F32),
            pltpu.VMEM((KEYS, 2 * ROWS), BF),
            pltpu.VMEM((KEYS, 2 * ROWS), BF),
            pltpu.VMEM((SLOTS, 2, T, D), F32),
            pltpu.VMEM((2 * ROWS, D), F32),
            pltpu.VMEM((NQ, 2, T, D), BF),
            pltpu.VMEM((DEPTH, 2, T, D), BF),
            pltpu.VMEM((2, T, D), BF),
            pltpu.VMEM((4, 2, T, D), BF),
            pltpu.VMEM((NQ, 2, T, D), BF),
            pltpu.VMEM((2, 2, D), F32),
            pltpu.VMEM((NQ, 2, D), F32),
            pltpu.VMEM((NX * NY, 2, D), F32),
            pltpu.VMEM((2, D), F32),
            dma((8,)),
            dma(()),
            dma((SLOTS,)),
            dma(()),
            dma(()),
            dma((2,)),
            dma(()),
            dma(()),
            dma(()),
            dma(()),
            dma(()),
            dma(()),
            dma(()),
            dma(()),
        ],
        compiler_params=pltpu.CompilerParams(
            collective_id=0, has_side_effects=True, vmem_limit_bytes=40 * 2**20
        ),
        cost_estimate=pl.CostEstimate(flops=10 * 2 * ROWS * KEYS * D, bytes_accessed=2**20, transcendentals=2 * ROWS * KEYS),
    )(
        *(
            pltpu.with_memory_space_constraint(array, pltpu.HBM)
            for array in (
                queries,
                keys,
                values,
                output_gradient,
                q_gain.reshape(1, D),
                k_gain.reshape(1, D),
                jnp.asarray(rope_table()),
            )
        ),
        leaf_len,
    )
    dq, dk, dv, dq_gain, dk_gain = pl.pallas_call(
        hand_over,
        name="hand_over",
        out_shape=[jax.ShapeDtypeStruct(r.shape, r.dtype) for r in results],
        in_specs=[anywhere] * 5,
        out_specs=[in_hbm] * 5,
        scratch_shapes=[dma((5,))],
        compiler_params=pltpu.CompilerParams(vmem_limit_bytes=8 * 2**20),
    )(*(pltpu.with_memory_space_constraint(r, pltpu.VMEM) for r in results))
    return dq, dk, dv, dq_gain.reshape(D), dk_gain.reshape(D)


def solution(mesh):
    shape = dict(mesh.shape)
    if shape != {"leaf": NX * NZ * NC, "head": NY}:
        raise ValueError("another mesh")
    split = P(None, "leaf", "head")
    return jax.shard_map(
        on_device,
        mesh=mesh,
        in_specs=(split, split, split, split, P(), P(), P("leaf")),
        out_specs=(split, split, split, P(), P()),
        check_vma=False,
    )
```

time: 38.4 us -> 34.1 us (0.89)
  Pallas kernels: 36.9 us -> 32.6 us
    pallas_call x1, Pallas kernels: 36.2 us -> 31.9 us  [on_device(): pl.pallas_call(kernel, name='tree_backward', out_shape=[pltpu.VMEM(querie...]
where the time goes in v3:
time: 34.1 us; the launch traced here: 33.9 us
  Pallas kernels  32.6 us (96%)
  between operations  1.29 us (4%)
    pallas_call x1, Pallas kernels, on_device(): pl.pallas_call(kernel, name='tree_backward', out_shape=[pltpu.VMEM(querie...  31.9 us
    pallas_call x1, Pallas kernels, on_device(): pl.pallas_call(hand_over, name='hand_over', out_shape=[jax.ShapeDtypeStru...  0.76 us

profile of v3, /device:TPU:1, one launch (start us, length us, event | category | flops | bytes accessed | tf_op | source)
XLA Modules:
  0.0 33.9 jit_solution(980224021895800266)
XLA Ops:
  1.3 31.9 %tree_backward.1 = (bf16[2,64,1024]{2,1,0:T(8,128)(2,1)S(1)}, bf16[2,64,128]{2,1,0:T(8,128)(2,1)S(1)}, bf16[2,64,128]{2,1,0:T(8,128)(2,1)S(1)}, f32[1,128]{1,0:T(1,128)S(1)}, f32[1,128]{1,0:T(1,128)S(1)}) custom-call(bf16[2,64,1024]{2,1,0:T(8,128)(2,1)} %q_in.1, bf16[2,64,128]{2,1,0:T(8,128)(2,1)} %k_in.1, bf16[2,64,128]{2,1,0:T(8,128)(2,1)} %v_in.1, ...), custom_call_target="tpu_custom_call" | custom-call | flops 587202560 | bytes 1048576 | tf_op jit(solution)/shard_map/tree_backward/pallas_call | solution.py:537
  33.2 0.8 %hand_over.1 = (bf16[2,64,1024]{2,1,0:T(8,128)(2,1)}, bf16[2,64,128]{2,1,0:T(8,128)(2,1)}, bf16[2,64,128]{2,1,0:T(8,128)(2,1)}, f32[1,128]{1,0:T(1,128)}, f32[1,128]{1,0:T(1,128)}) custom-call(bf16[2,64,1024]{2,1,0:T(8,128)(2,1)S(1)} %get-tuple-element.15.refs_0_, bf16[2,64,128]{2,1,0:T(8,128)(2,1)S(1)} %get-tuple-element.16.refs_1_, ...), custom_call_target="tpu_custom_call" | custom-call | tf_op jit(solution)/shard_map/hand_over/pallas_call | solution.py:615

commit v4 on v3

--- a/solution.py
+++ b/solution.py
@@ -95,9 +95,14 @@
     holder = {level: q // 2**level * 2**level + 2 ** (level - 1) for level in range(1, 5)}
     is_relay = q == 1
     is_near = q == 5
+    is_extra = jnp.logical_and(leaf == 3, y == 0)
     is_second = q == 9
     far_owner = jnp.logical_and(q == 0, x > 0)
     plane = x * NY + y
+    mirror = (NZ - 1 - z) * NC + c
+    low = jnp.where(z < 4, q, mirror)
+    sends_six = jnp.logical_or(z >= 4, x != 2)
+    sends_five = jnp.logical_or(z >= 4, lax.rem(x, 2) == 0)
 
     def among(places):
         here = q == places[0]
@@ -116,9 +121,13 @@
         def _(relay=relay):
             greet(at(x, relay))
 
-    @pl.when(z > 4)
+    @pl.when(among((10, 11, 12, 13)))
     def _():
         greet(at(x, 9))
+
+    @pl.when(z == NZ - 1)
+    def _():
+        greet(at(x, 13))
 
     @pl.when(jnp.logical_or(z < 4, is_second))
     def _():
@@ -135,13 +144,23 @@
         greet(at(2, 0))
         greet(at(x // 2 * 2 + 1, 0))
 
-    for other in range(1, NX):
-        greet(at(lax.rem(x + other, NX), q))
-
-    early = jnp.int32(NX - 1)
-    early = early + jnp.where(c == 1, 1, 0)
-    early = early + jnp.where(is_relay, 3 + NX * NY - 1, 0) + jnp.where(is_near, 3, 0)
-    early = early + jnp.where(is_second, 6, 0)
+    @pl.when(jnp.logical_and(z < 4, x == 2))
+    def _():
+        for xx in range(NX):
+            greet(at(xx, mirror))
+        for xx in (0, 1, 3):
+            greet(at(xx, q))
+
+    @pl.when(jnp.logical_and(z < 4, lax.rem(x, 2) == 1))
+    def _():
+        greet(at(x, mirror))
+        greet(at(x - 1, mirror))
+        greet(at(x - 1, q))
+
+    early = jnp.where(c == 1, 1, 0)
+    early = early + jnp.where(sends_six, 1, 0) + jnp.where(sends_five, 1, 0)
+    early = early + jnp.where(is_relay, 3 + NX * NY, 0) + jnp.where(is_near, 3, 0)
+    early = early + jnp.where(is_second, 4, 0) + jnp.where(q == 13, 2, 0)
     for level, count in ((2, 3), (3, 7), (4, 9), (5, 4), (6, 2 * NX)):
         early = early + jnp.where(hosted == level, count, 0)
 
@@ -168,6 +187,14 @@
 
         lax.fori_loop(1, NX * NY, greet_plane, 0)
 
+    @pl.when(is_extra)
+    def _():
+        def greet_all(n, carry):
+            greet(at(n // NY, 1, lax.rem(n, NY)))
+            return carry
+
+        lax.fori_loop(0, NX * NY, greet_all, 0)
+
     settle(1, load_sem.at[0])
 
     pl.semaphore_wait(barrier, early)
@@ -200,7 +227,7 @@
     @pl.when(is_second)
     def _():
         remote(own, kv.at[4], b_send, b_recv.at[4], at(x, 8)).wait_recv()
-        for qq in (15, 14, 13, 12, 11, 10):
+        for qq in (13, 12, 10, 11):
             remote(kv.at[4], kv.at[4], b_send, b_recv.at[4], at(x, qq)).start()
 
     top_two = kv.at[pl.ds(5, 2)]
@@ -251,13 +278,24 @@
         v_all[rows, :] = kv[slot, 1]
 
     def from_holder(level):
-        @pl.when(jnp.logical_and(q != holder[level], jnp.logical_not(jnp.logical_and(is_second, level == 4))))
+        @pl.when(jnp.logical_and(q != holder[level], jnp.logical_not(jnp.logical_and(among((9, 13)), level == 4))))
         def _():
             remote(own, kv.at[level], b_send, b_recv.at[level], at(x, holder[level])).wait_recv()
 
         @pl.when(hosted == level)
         def _():
             settle(1, load_sem.at[7])
+
+    @pl.when(q == 13)
+    def _():
+        remote(own, kv.at[4], b_send, b_recv.at[4], at(x, 9)).wait_recv()
+        for qq in (14, 15):
+            remote(kv.at[4], kv.at[4], b_send, b_recv.at[4], at(x, qq)).start()
+
+    @pl.when(jnp.logical_and(c == 1, jnp.logical_not(jnp.logical_or(is_relay, is_near))))
+    def _():
+        remote(top_two, top_two, b_send, b_recv.at[5], at(x, 1)).wait_recv()
+        remote(top_two, top_two, b_send, b_recv.at[5], at(x, q - 1)).start()
 
     take(0)
     for level in (1, 2, 3):
@@ -301,13 +339,9 @@
         rows = slice(kind * ROWS, (kind + 1) * ROWS)
         near_e[:, rows], near_d[:, rows], near_s[0:1, rows], near_s[1:2, rows], near_s[2:3, rows] = partial(0, NEAR, kind)
 
-    @pl.when(jnp.logical_not(jnp.logical_or(is_relay, is_near)))
+    @pl.when(c == 0)
     def _():
         remote(top_two, top_two, b_send, b_recv.at[5], at(x, 1)).wait_recv()
-
-        @pl.when(c == 1)
-        def _():
-            remote(top_two, top_two, b_send, b_recv.at[5], at(x, q - 1)).start()
 
     take(5)
     take(6)
@@ -339,15 +373,6 @@
     for slot in range(1, SLOTS):
         send_kv[slot - 1] = part[slot].astype(BF)
 
-    @pl.when(x != 2)
-    def _():
-        n = jnp.minimum(x, 2)
-        remote(send_kv.at[5], x_recv.at[n], x_sem.at[0], xr_sem, at(2, q)).start()
-
-    @pl.when(lax.rem(x, 2) == 0)
-    def _():
-        remote(send_kv.at[4], x_recv.at[3], x_sem.at[1], xr_sem, at(x + 1, q)).start()
-
     straight, crossed = dq_turned * wq_cos[...], dq_turned * wq_sin[...]
     both = straight - jnp.concatenate([crossed[D // 2 :], crossed[: D // 2]], axis=0)
     lanes = both[:, :D]
@@ -364,6 +389,16 @@
     def _():
         remote(gain_send.at[0], gain_z.at[lax.rem(q + NQ - 2, NQ)], gz_send, gz_recv, at(x, 1)).start()
 
+    @pl.when(sends_six)
+    def _():
+        n = jnp.where(z >= 4, x, NX + jnp.minimum(x, 2))
+        remote(send_kv.at[5], x_recv.at[n], x_sem.at[0], xr_sem, at(2, low)).start()
+
+    @pl.when(sends_five)
+    def _():
+        n = jnp.where(z >= 4, 1 + lax.rem(x, 2), 0)
+        remote(send_kv.at[4], x_recv.at[n], x_sem.at[1], xr_sem, at(x // 2 * 2 + 1, low)).start()
+
     for level in range(1, 5):
 
         @pl.when(q != holder[level])
@@ -394,63 +429,6 @@
     dk_out[0] = key_gradient(kv[0, 0], part[0, 0], DEPTH * T)
     dv_out[0] = part[0, 1].astype(BF)
 
-    @pl.when(x == 2)
-    def _():
-        settle(3, xr_sem)
-        total = part[6]
-        for n in range(3):
-            total = total + x_recv[n].astype(F32)
-        part[6] = total
-        send_sum[...] = total.astype(BF)
-
-    @pl.when(lax.rem(x, 2) == 1)
-    def _():
-        settle(1, xr_sem)
-        total = part[5] + x_recv[3].astype(F32)
-        part[5] = total
-        send_sum[...] = total.astype(BF)
-
-    @pl.when(jnp.logical_and(x > 0, q != 0))
-    def _():
-        remote(send_sum, z_recv.at[q - 1], s_send, r_recv, at(x, 0)).start()
-
-    @pl.when(among((1, 5, 9)))
-    def _():
-        settle(9, b_send)
-
-    @pl.when(among((3, 7, 11, 13, 15)))
-    def _():
-        settle(3, b_send)
-
-    for level, count in ((2, 3), (3, 7), (4, 9), (5, 4), (6, 2 * NX)):
-
-        @pl.when(hosted == level)
-        def _(count=count):
-            settle(count, b_send)
-
-    @pl.when(hosted <= DEPTH)
-    def _():
-        size = jnp.int32(NQ)
-        for level in range(1, 4):
-            size = jnp.where(hosted == level, 2**level, size)
-        for level in range(1, DEPTH + 1):
-
-            @pl.when(hosted == level)
-            def _(level=level):
-                settle(2 ** min(level, 4) - 1, r_recv)
-
-        def add(n, total):
-            return total + z_recv[n].astype(F32)
-
-        total = lax.fori_loop(0, size - 1, add, part[hosted])
-        dk_out[1] = key_gradient(own[0], total[0], pl.multiple_of(place[1], T))
-        dv_out[1] = total[1].astype(BF)
-
-    @pl.when(hosted > DEPTH)
-    def _():
-        dk_out[1] = jnp.zeros((T, D), BF)
-        dv_out[1] = jnp.zeros((T, D), BF)
-
     @pl.when(is_relay)
     def _():
         gain_z[NQ - 1] = terms
@@ -464,41 +442,76 @@
         for dx, dy in AWAY:
             device = at(lax.rem(x + dx, NX), 1, lax.rem(y + dy, NY))
             remote(gain_send.at[1], gain_p.at[plane], gp_send, gp_recv, device).start()
-
-        away = gain_p.at[pl.ds(0, len(AWAY))]
-        pltpu.make_async_copy(away, away, gp_recv).wait()
+        remote(gain_send.at[1], gain_p.at[plane], gp_send, gp_recv, at(0, 3, 0)).start()
+
+    def gather(level, count):
+        settle(count, xr_sem)
+        total = part[level]
+        for n in range(count):
+            total = total + x_recv[n].astype(F32)
+        part[level] = total
+        send_sum[...] = total.astype(BF)
+
+    @pl.when(jnp.logical_and(z < 4, x == 2))
+    def _():
+        gather(6, 2 * NX - 1)
+
+    @pl.when(jnp.logical_and(z < 4, lax.rem(x, 2) == 1))
+    def _():
+        gather(5, 3)
+
+    sums = jnp.logical_and(x > 0, jnp.logical_and(z < 4, q != 0))
+
+    @pl.when(sums)
+    def _():
+        remote(send_sum, z_recv.at[q - 1], s_send, r_recv, at(x, 0)).start()
+
+    for places, count in (((1, 5), 9), ((9,), 7), ((13,), 5)):
+
+        @pl.when(among(places))
+        def _(count=count):
+            settle(count, b_send)
+
+    @pl.when(among((3, 7, 11, 15)))
+    def _():
+        settle(3, b_send)
+
+    for level, count in ((2, 3), (3, 7), (4, 9), (5, 4), (6, 2 * NX)):
+
+        @pl.when(hosted == level)
+        def _(count=count):
+            settle(count, b_send)
+
+    @pl.when(hosted <= DEPTH)
+    def _():
+        size = jnp.int32(NQ)
+        for level, count in ((1, 2), (2, 4), (3, 8), (5, 8), (6, 8)):
+            size = jnp.where(hosted == level, count, size)
+        for level in range(1, DEPTH + 1):
+
+            @pl.when(hosted == level)
+            def _(level=level):
+                settle(2**level - 1 if level < 5 else NQ // 2 - 1, r_recv)
+
+        def add(n, total):
+            return total + z_recv[n].astype(F32)
+
+        total = lax.fori_loop(0, size - 1, add, part[hosted])
+        dk_out[1] = key_gradient(own[0], total[0], pl.multiple_of(place[1], T))
+        dv_out[1] = total[1].astype(BF)
+
+    @pl.when(hosted > DEPTH)
+    def _():
+        dk_out[1] = jnp.zeros((T, D), BF)
+        dv_out[1] = jnp.zeros((T, D), BF)
+
+    def total_of_lines(senders):
+        lines = gain_p.at[pl.ds(0, senders)]
+        pltpu.make_async_copy(lines, lines, gp_recv).wait()
         total = gain_p[0]
         for n in range(1, NX * NY):
             total = total + gain_p[n]
         gain_total[...] = total
-        for qq in (3, 5, 0):
-            remote(gain_total, gain_total, gt_send, gt_recv, at(x, qq)).start()
-        pltpu.make_async_copy(away, away, gp_send).wait()
-
-    @pl.when(x != 2)
-    def _():
-        settle(1, x_sem.at[0])
-
-    @pl.when(lax.rem(x, 2) == 0)
-    def _():
-        settle(1, x_sem.at[1])
-
-    @pl.when(hosted < 5)
-    def _():
-        settle(3, r_send)
-
-    @pl.when(hosted >= 5)
-    def _():
-        settle(4, r_send)
-
-    @pl.when(jnp.logical_and(x > 0, q != 0))
-    def _():
-        settle(1, s_send)
-
-    @pl.when(jnp.logical_not(is_relay))
-    def _():
-        pltpu.make_async_copy(gain_total, gain_total, gz_send).wait()
-        pltpu.make_async_copy(gain_total, gain_total, gt_recv).wait()
 
     def pass_on(when, targets):
         @pl.when(when)
@@ -506,9 +519,52 @@
             for qq in targets:
                 remote(gain_total, gain_total, gt_send, gt_recv, at(x, qq)).start()
 
-    pass_on(q == 0, (15, 13, 11))
-    pass_on(q == 5, (7, 9, 4))
-    pass_on(jnp.logical_and(c == 1, jnp.logical_and(q != 5, q != 1)), (q - 1,))
+    @pl.when(is_relay)
+    def _():
+        total_of_lines(NX * NY - 1)
+
+    @pl.when(is_extra)
+    def _():
+        total_of_lines(NX * NY)
+
+    pass_on(jnp.logical_and(is_relay, plane > 0), (3, 5, 0))
+    pass_on(is_extra, (5, 2, 0))
+
+    @pl.when(is_relay)
+    def _():
+        pltpu.make_async_copy(gain_p, gain_p, gp_send).wait()
+
+    @pl.when(sends_six)
+    def _():
+        settle(1, x_sem.at[0])
+
+    @pl.when(sends_five)
+    def _():
+        settle(1, x_sem.at[1])
+
+    @pl.when(hosted < 5)
+    def _():
+        settle(3, r_send)
+
+    @pl.when(hosted >= 5)
+    def _():
+        settle(4, r_send)
+
+    @pl.when(sums)
+    def _():
+        settle(1, s_send)
+
+    @pl.when(jnp.logical_not(is_relay))
+    def _():
+        pltpu.make_async_copy(gain_total, gain_total, gz_send).wait()
+
+        @pl.when(jnp.logical_not(is_extra))
+        def _():
+            pltpu.make_async_copy(gain_total, gain_total, gt_recv).wait()
+
+    pass_one = jnp.logical_and(among((3, 7, 9, 11, 13, 15)), jnp.logical_not(is_extra))
+    pass_on(q == 5, (7, 9, 11, 13, 15, 4))
+    pass_on(pass_one, (q - 1,))
     dqg_out[...] = gain_total[0:1]
     dkg_out[...] = gain_total[1:2]
 
@@ -518,8 +574,9 @@
             sent = gain_z.at[pl.ds(0, count)]
             pltpu.make_async_copy(sent, sent, gt_send).wait()
 
-    passed(jnp.logical_or(q < 2, q == 5), 3)
-    passed(jnp.logical_and(c == 1, jnp.logical_and(q != 5, q != 1)), 1)
+    passed(jnp.logical_or(is_extra, jnp.logical_and(is_relay, plane > 0)), 3)
+    passed(q == 5, 6)
+    passed(pass_one, 1)
 
 
 def hand_over(*refs):
@@ -572,7 +629,7 @@
             pltpu.VMEM((NQ, 2, T, D), BF),
             pltpu.VMEM((DEPTH, 2, T, D), BF),
             pltpu.VMEM((2, T, D), BF),
-            pltpu.VMEM((4, 2, T, D), BF),
+            pltpu.VMEM((2 * NX - 1, 2, T, D), BF),
             pltpu.VMEM((NQ, 2, T, D), BF),
             pltpu.VMEM((2, 2, D), F32),
             pltpu.VMEM((NQ, 2, D), F32),

time: 34.1 us -> 33.2 us (0.974)
  Pallas kernels: 32.6 us -> 31.7 us
    pallas_call x1, Pallas kernels: 31.9 us -> 30.9 us  [on_device(): pl.pallas_call(kernel, name='tree_backward', out_shape=[pltpu.VMEM(querie...]
where the time goes in v4:
time: 33.2 us; the launch traced here: 33 us
  Pallas kernels  31.7 us (95%)
  between operations  1.29 us (4%)
    pallas_call x1, Pallas kernels, on_device(): pl.pallas_call(kernel, name='tree_backward', out_shape=[pltpu.VMEM(querie...  30.9 us
    pallas_call x1, Pallas kernels, on_device(): pl.pallas_call(hand_over, name='hand_over', out_shape=[jax.ShapeDtypeStru...  0.76 us

profile of v4, /device:TPU:1, one launch (start us, length us, event | category | flops | bytes accessed | tf_op | source)
XLA Modules:
  0.0 33.0 jit_solution(7078016040162808950)
XLA Ops:
  1.3 30.9 %tree_backward.1 = (bf16[2,64,1024]{2,1,0:T(8,128)(2,1)S(1)}, bf16[2,64,128]{2,1,0:T(8,128)(2,1)S(1)}, bf16[2,64,128]{2,1,0:T(8,128)(2,1)S(1)}, f32[1,128]{1,0:T(1,128)S(1)}, f32[1,128]{1,0:T(1,128)S(1)}) custom-call(bf16[2,64,1024]{2,1,0:T(8,128)(2,1)} %q_in.1, bf16[2,64,128]{2,1,0:T(8,128)(2,1)} %k_in.1, bf16[2,64,128]{2,1,0:T(8,128)(2,1)} %v_in.1, ...), custom_call_target="tpu_custom_call" | custom-call | flops 587202560 | bytes 1048576 | tf_op jit(solution)/shard_map/tree_backward/pallas_call | solution.py:594
  32.2 0.8 %hand_over.1 = (bf16[2,64,1024]{2,1,0:T(8,128)(2,1)}, bf16[2,64,128]{2,1,0:T(8,128)(2,1)}, bf16[2,64,128]{2,1,0:T(8,128)(2,1)}, f32[1,128]{1,0:T(1,128)}, f32[1,128]{1,0:T(1,128)}) custom-call(bf16[2,64,1024]{2,1,0:T(8,128)(2,1)S(1)} %get-tuple-element.15.refs_0_, bf16[2,64,128]{2,1,0:T(8,128)(2,1)S(1)} %get-tuple-element.16.refs_1_, ...), custom_call_target="tpu_custom_call" | custom-call | tf_op jit(solution)/shard_map/hand_over/pallas_call | solution.py:672

commit v5 on v4

--- a/solution.py
+++ b/solution.py
@@ -16,6 +16,7 @@
 SLOTS = DEPTH + 1
 KEYS = SLOTS * T
 NEAR = 4
+MID = 5
 ROWS = G * T
 NX, NZ, NC, NY = 4, 8, 2, 8
 NQ = NZ * NC
@@ -23,7 +24,7 @@
 BF = jnp.bfloat16
 F32 = jnp.float32
 MESH = pl.DeviceIdType.MESH
-SERVED = ((1, (13, 15, 3)), (5, (11, 9, 7)))
+SERVED = ((1, (11, 13, 15, 3)), (5, (9, 7)))
 AWAY = sorted(
     ((dx, dy) for dx in range(NX) for dy in range(NY) if dx or dy),
     key=lambda step: -min(step[0], NX - step[0]) - min(step[1], NY - step[1]),
@@ -115,6 +116,11 @@
     def greet(device):
         pl.semaphore_signal(barrier, inc=1, device_id=device, device_id_type=MESH)
 
+    @pl.when(jnp.logical_or(is_relay, is_near))
+    def _():
+        greet(at(2, 0))
+        greet(at(x // 2 * 2 + 1, 0))
+
     for relay, served in SERVED:
 
         @pl.when(among(served))
@@ -135,14 +141,9 @@
 
     for level in (3, 2, 1):
 
-        @pl.when(q != holder[level])
+        @pl.when(jnp.logical_and(q != holder[level], jnp.logical_not(jnp.logical_and(z == NZ - 1, level == 3))))
         def _(level=level):
             greet(at(x, holder[level]))
-
-    @pl.when(jnp.logical_or(is_relay, is_near))
-    def _():
-        greet(at(2, 0))
-        greet(at(x // 2 * 2 + 1, 0))
 
     @pl.when(jnp.logical_and(z < 4, x == 2))
     def _():
@@ -159,8 +160,8 @@
 
     early = jnp.where(c == 1, 1, 0)
     early = early + jnp.where(sends_six, 1, 0) + jnp.where(sends_five, 1, 0)
-    early = early + jnp.where(is_relay, 3 + NX * NY, 0) + jnp.where(is_near, 3, 0)
-    early = early + jnp.where(is_second, 4, 0) + jnp.where(q == 13, 2, 0)
+    early = early + jnp.where(is_relay, 4 + NX * NY, 0) + jnp.where(is_near, 2, 0)
+    early = early + jnp.where(is_second, 4, 0) + jnp.where(q == 13, 2, 0) - jnp.where(q == 12, 2, 0)
     for level, count in ((2, 3), (3, 7), (4, 9), (5, 4), (6, 2 * NX)):
         early = early + jnp.where(hosted == level, count, 0)
 
@@ -220,7 +221,14 @@
             if level == 4:
                 offsets = [1] + [o for o in offsets if o < 0]
             for offset in offsets:
-                remote(own, kv.at[level], b_send, b_recv.at[level], at(x, q + offset)).start()
+                if level == 3 and offset in (2, 3):
+
+                    @pl.when(q != 12)
+                    def _(offset=offset):
+                        remote(own, kv.at[level], b_send, b_recv.at[level], at(x, q + offset)).start()
+
+                else:
+                    remote(own, kv.at[level], b_send, b_recv.at[level], at(x, q + offset)).start()
             for n in range(2):
                 pltpu.make_async_copy((k_in, v_in)[n].at[1], kv.at[level, n], load_sem.at[7]).start()
 
@@ -278,7 +286,9 @@
         v_all[rows, :] = kv[slot, 1]
 
     def from_holder(level):
-        @pl.when(jnp.logical_and(q != holder[level], jnp.logical_not(jnp.logical_and(among((9, 13)), level == 4))))
+        passed_on = {3: q == 13, 4: among((9, 13))}.get(level, False)
+
+        @pl.when(jnp.logical_and(q != holder[level], jnp.logical_not(passed_on)))
         def _():
             remote(own, kv.at[level], b_send, b_recv.at[level], at(x, holder[level])).wait_recv()
 
@@ -288,6 +298,17 @@
 
     @pl.when(q == 13)
     def _():
+        remote(own, kv.at[3], b_send, b_recv.at[3], at(x, 12)).wait_recv()
+        for qq in (14, 15):
+            remote(kv.at[3], kv.at[3], b_send, b_recv.at[3], at(x, qq)).start()
+
+    take(0)
+    for level in (1, 2):
+        from_holder(level)
+        take(level)
+
+    @pl.when(q == 13)
+    def _():
         remote(own, kv.at[4], b_send, b_recv.at[4], at(x, 9)).wait_recv()
         for qq in (14, 15):
             remote(kv.at[4], kv.at[4], b_send, b_recv.at[4], at(x, qq)).start()
@@ -297,10 +318,8 @@
         remote(top_two, top_two, b_send, b_recv.at[5], at(x, 1)).wait_recv()
         remote(top_two, top_two, b_send, b_recv.at[5], at(x, q - 1)).start()
 
-    take(0)
-    for level in (1, 2, 3):
-        from_holder(level)
-        take(level)
+    from_holder(3)
+    take(3)
 
     key_at = lax.broadcasted_iota(jnp.int32, (T, ROWS), 0)
     row_at = lax.rem(lax.broadcasted_iota(jnp.int32, (T, ROWS), 1), T)
@@ -335,9 +354,22 @@
             jnp.sum(raised * dprobs, axis=0, keepdims=True),
         )
 
+    def keep(first, last, at_row, kind, rows):
+        raised, products, *sums = partial(first, last, kind)
+        near_e[first * T : last * T, rows] = raised
+        near_d[first * T : last * T, rows] = products
+        for n, line in enumerate(sums):
+            near_s[at_row + n : at_row + n + 1, rows] = line
+
     for kind in range(2):
         rows = slice(kind * ROWS, (kind + 1) * ROWS)
-        near_e[:, rows], near_d[:, rows], near_s[0:1, rows], near_s[1:2, rows], near_s[2:3, rows] = partial(0, NEAR, kind)
+        keep(0, NEAR, 0, kind, rows)
+
+    from_holder(4)
+    take(4)
+    for kind in range(2):
+        rows = slice(kind * ROWS, (kind + 1) * ROWS)
+        keep(NEAR, MID, 3, kind, rows)
 
     @pl.when(c == 0)
     def _():
@@ -345,34 +377,25 @@
 
     take(5)
     take(6)
-    from_holder(4)
-    take(4)
-
     for kind in range(2):
         rows = slice(kind * ROWS, (kind + 1) * ROWS)
-        far_e, far_d, far_top, far_sum, far_delta = partial(NEAR, SLOTS, kind)
-        near_top = near_s[0:1, rows]
-        top = jnp.maximum(near_top, far_top)
-        near_f, far_f = jnp.exp(near_top - top), jnp.exp(far_top - top)
-        over = 1.0 / (near_s[1:2, rows] * near_f + far_sum * far_f)
-        near_f, far_f = near_f * over, far_f * over
-        delta = near_s[2:3, rows] * near_f + far_delta * far_f
-        near = near_e[:, rows] * near_f
-        far = far_e * far_f
-        probs[: NEAR * T, rows] = near.astype(BF)
-        probs[NEAR * T :, rows] = far.astype(BF)
-        dscores[: NEAR * T, rows] = (near * (near_d[:, rows] - delta)).astype(BF)
-        dscores[NEAR * T :, rows] = (far * (far_d - delta)).astype(BF)
+        far_e, far_d, far_top, far_sum, far_delta = partial(MID, SLOTS, kind)
+        near_top, mid_top = near_s[0:1, rows], near_s[3:4, rows]
+        top = jnp.maximum(jnp.maximum(near_top, mid_top), far_top)
+        near_f, mid_f, far_f = jnp.exp(near_top - top), jnp.exp(mid_top - top), jnp.exp(far_top - top)
+        over = 1.0 / (near_s[1:2, rows] * near_f + near_s[4:5, rows] * mid_f + far_sum * far_f)
+        near_f, mid_f, far_f = near_f * over, mid_f * over, far_f * over
+        delta = near_s[2:3, rows] * near_f + near_s[5:6, rows] * mid_f + far_delta * far_f
+        for first, last, factor, e, d in (
+            (0, NEAR, near_f, near_e[: NEAR * T, rows], near_d[: NEAR * T, rows]),
+            (NEAR, MID, mid_f, near_e[NEAR * T :, rows], near_d[NEAR * T :, rows]),
+            (MID, SLOTS, far_f, far_e, far_d),
+        ):
+            prob = e * factor
+            probs[first * T : last * T, rows] = prob.astype(BF)
+            dscores[first * T : last * T, rows] = (prob * (d - delta)).astype(BF)
     dk_all = dot(dscores[...], q_rot[...], ((1,), (0,))) * SCALE
-    dv_all = dot(probs[...], g_rows[...], ((1,), (0,)))
     dq_turned = dot(k_rot[...], dscores[...], ((0,), (0,))) * SCALE
-    for slot in range(SLOTS):
-        part[slot, 0] = dk_all[slot * T : (slot + 1) * T]
-        part[slot, 1] = dv_all[slot * T : (slot + 1) * T]
-
-    for slot in range(1, SLOTS):
-        send_kv[slot - 1] = part[slot].astype(BF)
-
     straight, crossed = dq_turned * wq_cos[...], dq_turned * wq_sin[...]
     both = straight - jnp.concatenate([crossed[D // 2 :], crossed[: D // 2]], axis=0)
     lanes = both[:, :D]
@@ -388,6 +411,14 @@
     @pl.when(jnp.logical_not(is_relay))
     def _():
         remote(gain_send.at[0], gain_z.at[lax.rem(q + NQ - 2, NQ)], gz_send, gz_recv, at(x, 1)).start()
+
+    dv_all = dot(probs[...], g_rows[...], ((1,), (0,)))
+    for slot in range(SLOTS):
+        part[slot, 0] = dk_all[slot * T : (slot + 1) * T]
+        part[slot, 1] = dv_all[slot * T : (slot + 1) * T]
+
+    for slot in range(1, SLOTS):
+        send_kv[slot - 1] = part[slot].astype(BF)
 
     @pl.when(sends_six)
     def _():
@@ -466,7 +497,7 @@
     def _():
         remote(send_sum, z_recv.at[q - 1], s_send, r_recv, at(x, 0)).start()
 
-    for places, count in (((1, 5), 9), ((9,), 7), ((13,), 5)):
+    for places, count in (((1,), 11), ((5, 9, 13), 7), ((4,), 7), ((12,), 5)):
 
         @pl.when(among(places))
         def _(count=count):
@@ -476,7 +507,7 @@
     def _():
         settle(3, b_send)
 
-    for level, count in ((2, 3), (3, 7), (4, 9), (5, 4), (6, 2 * NX)):
+    for level, count in ((2, 3), (4, 9), (5, 4), (6, 2 * NX)):
 
         @pl.when(hosted == level)
         def _(count=count):
@@ -527,8 +558,8 @@
     def _():
         total_of_lines(NX * NY)
 
-    pass_on(jnp.logical_and(is_relay, plane > 0), (3, 5, 0))
-    pass_on(is_extra, (5, 2, 0))
+    pass_on(jnp.logical_and(is_relay, plane > 0), (3, 5, 7, 0))
+    pass_on(is_extra, (5, 7, 2, 0))
 
     @pl.when(is_relay)
     def _():
@@ -563,7 +594,7 @@
             pltpu.make_async_copy(gain_total, gain_total, gt_recv).wait()
 
     pass_one = jnp.logical_and(among((3, 7, 9, 11, 13, 15)), jnp.logical_not(is_extra))
-    pass_on(q == 5, (7, 9, 11, 13, 15, 4))
+    pass_on(q == 5, (9, 11, 13, 15, 4))
     pass_on(pass_one, (q - 1,))
     dqg_out[...] = gain_total[0:1]
     dkg_out[...] = gain_total[1:2]
@@ -574,8 +605,8 @@
             sent = gain_z.at[pl.ds(0, count)]
             pltpu.make_async_copy(sent, sent, gt_send).wait()
 
-    passed(jnp.logical_or(is_extra, jnp.logical_and(is_relay, plane > 0)), 3)
-    passed(q == 5, 6)
+    passed(jnp.logical_or(is_extra, jnp.logical_and(is_relay, plane > 0)), 4)
+    passed(q == 5, 5)
     passed(pass_one, 1)
 
 
@@ -619,8 +650,8 @@
             pltpu.VMEM((D, 2 * ROWS), F32),
             pltpu.VMEM((KEYS, D), F32),
             pltpu.VMEM((KEYS, D), F32),
-            pltpu.VMEM((NEAR * T, 2 * ROWS), F32),
-            pltpu.VMEM((NEAR * T, 2 * ROWS), F32),
+            pltpu.VMEM((MID * T, 2 * ROWS), F32),
+            pltpu.VMEM((MID * T, 2 * ROWS), F32),
             pltpu.VMEM((8, 2 * ROWS), F32),
             pltpu.VMEM((KEYS, 2 * ROWS), BF),
             pltpu.VMEM((KEYS, 2 * ROWS), BF),

time: 33.2 us -> 32.3 us (0.973)
  Pallas kernels: 31.7 us -> 30.8 us
    pallas_call x1, Pallas kernels: 30.9 us -> 30 us  [on_device(): pl.pallas_call(kernel, name='tree_backward', out_shape=[pltpu.VMEM(querie...]
where the time goes in v5:
time: 32.3 us; the launch traced here: 32.1 us
  Pallas kernels  30.8 us (95%)
  between operations  1.29 us (4%)
    pallas_call x1, Pallas kernels, on_device(): pl.pallas_call(kernel, name='tree_backward', out_shape=[pltpu.VMEM(querie...  30 us
    pallas_call x1, Pallas kernels, on_device(): pl.pallas_call(hand_over, name='hand_over', out_shape=[jax.ShapeDtypeStru...  0.76 us

profile of v5, /device:TPU:1, one launch (start us, length us, event | category | flops | bytes accessed | tf_op | source)
XLA Modules:
  0.0 32.1 jit_solution(4148374794092499903)
XLA Ops:
  1.3 30.0 %tree_backward.1 = (bf16[2,64,1024]{2,1,0:T(8,128)(2,1)S(1)}, bf16[2,64,128]{2,1,0:T(8,128)(2,1)S(1)}, bf16[2,64,128]{2,1,0:T(8,128)(2,1)S(1)}, f32[1,128]{1,0:T(1,128)S(1)}, f32[1,128]{1,0:T(1,128)S(1)}) custom-call(bf16[2,64,1024]{2,1,0:T(8,128)(2,1)} %q_in.1, bf16[2,64,128]{2,1,0:T(8,128)(2,1)} %k_in.1, bf16[2,64,128]{2,1,0:T(8,128)(2,1)} %v_in.1, ...), custom_call_target="tpu_custom_call" | custom-call | flops 587202560 | bytes 1048576 | tf_op jit(solution)/shard_map/tree_backward/pallas_call | solution.py:625
  31.3 0.8 %hand_over.1 = (bf16[2,64,1024]{2,1,0:T(8,128)(2,1)}, bf16[2,64,128]{2,1,0:T(8,128)(2,1)}, bf16[2,64,128]{2,1,0:T(8,128)(2,1)}, f32[1,128]{1,0:T(1,128)}, f32[1,128]{1,0:T(1,128)}) custom-call(bf16[2,64,1024]{2,1,0:T(8,128)(2,1)S(1)} %get-tuple-element.15.refs_0_, bf16[2,64,128]{2,1,0:T(8,128)(2,1)S(1)} %get-tuple-element.16.refs_1_, ...), custom_call_target="tpu_custom_call" | custom-call | tf_op jit(solution)/shard_map/hand_over/pallas_call | solution.py:703

commit v6 on v5

--- a/solution.py
+++ b/solution.py
@@ -24,6 +24,9 @@
 BF = jnp.bfloat16
 F32 = jnp.float32
 MESH = pl.DeviceIdType.MESH
+FIRST = ((0, 1, 0), (0, 3, 0), (0, 1, 1), (1, 1, 0), (2, 1, 0), (3, 1, 0))
+LAST_Y = (4, 5)
+EARLY_Q = 6
 SERVED = ((1, (11, 13, 15, 3)), (5, (9, 7)))
 AWAY = sorted(
     ((dx, dy) for dx in range(NX) for dy in range(NY) if dx or dy),
@@ -66,9 +69,9 @@
     dq_out, dk_out, dv_out, dqg_out, dkg_out,
     q_raw, g_raw, own, kv, qg, kg, table,
     q_rot, g_rows, k_rot, v_all, wq_cos, wq_sin, wk_cos, wk_sin, near_e, near_d, near_s, probs, dscores, part, y_q, ballast,
-    send_kv, send_sum, x_recv, z_recv, gain_send, gain_z, gain_p, gain_total,
+    send_kv, send_sum, x_recv, z_recv, gain_send, gain_z, gain_p, gain_d, gain_total,
     load_sem, b_send, b_recv, r_send, r_recv, x_sem, xr_sem, s_send,
-    gz_send, gz_recv, gp_send, gp_recv, gt_send, gt_recv,
+    gz_send, gz_recv, gp_send, gp_recv, gd_send, gd_recv, gt_send, gt_recv,
 ):
     leaf = lax.axis_index("leaf")
     y = lax.axis_index("head")
@@ -97,9 +100,12 @@
     is_relay = q == 1
     is_near = q == 5
     is_extra = jnp.logical_and(leaf == 3, y == 0)
+    is_first = jnp.logical_or(is_extra, jnp.logical_and(is_relay, jnp.logical_or(y == 0, jnp.logical_and(x == 0, y == 1))))
     is_second = q == 9
     far_owner = jnp.logical_and(q == 0, x > 0)
     plane = x * NY + y
+    starts_last = jnp.logical_and(y >= LAST_Y[0], y <= LAST_Y[-1])
+    direct = jnp.logical_and(starts_last, q >= EARLY_Q)
     mirror = (NZ - 1 - z) * NC + c
     low = jnp.where(z < 4, q, mirror)
     sends_six = jnp.logical_or(z >= 4, x != 2)
@@ -160,7 +166,7 @@
 
     early = jnp.where(c == 1, 1, 0)
     early = early + jnp.where(sends_six, 1, 0) + jnp.where(sends_five, 1, 0)
-    early = early + jnp.where(is_relay, 4 + NX * NY, 0) + jnp.where(is_near, 2, 0)
+    early = early + jnp.where(is_relay, 4 + NX * NY, 0) + jnp.where(is_near, 2 + jnp.where(starts_last, len(FIRST), 0), 0)
     early = early + jnp.where(is_second, 4, 0) + jnp.where(q == 13, 2, 0) - jnp.where(q == 12, 2, 0)
     for level, count in ((2, 3), (3, 7), (4, 9), (5, 4), (6, 2 * NX)):
         early = early + jnp.where(hosted == level, count, 0)
@@ -195,6 +201,12 @@
             return carry
 
         lax.fori_loop(0, NX * NY, greet_all, 0)
+
+    @pl.when(is_first)
+    def _():
+        for xx in range(NX):
+            for yy in LAST_Y:
+                greet(at(xx, 5, yy))
 
     settle(1, load_sem.at[0])
 
@@ -408,9 +420,16 @@
     terms = jnp.concatenate([gain_q, gain_k], axis=0)
     gain_send[0] = terms
 
+    @pl.when(direct)
+    def _():
+        for xx, qq, yy in FIRST:
+            slot = gain_d.at[x * len(LAST_Y) + y - LAST_Y[0], q - EARLY_Q]
+            remote(gain_send.at[0], slot, gd_send, gd_recv, at(xx, qq, yy)).start()
+
     @pl.when(jnp.logical_not(is_relay))
     def _():
-        remote(gain_send.at[0], gain_z.at[lax.rem(q + NQ - 2, NQ)], gz_send, gz_recv, at(x, 1)).start()
+        recv = gz_recv.at[jnp.where(q < EARLY_Q, 0, 1)]
+        remote(gain_send.at[0], gain_z.at[lax.rem(q + NQ - 2, NQ)], gz_send, recv, at(x, 1)).start()
 
     dv_all = dot(probs[...], g_rows[...], ((1,), (0,)))
     for slot in range(SLOTS):
@@ -462,18 +481,37 @@
 
     @pl.when(is_relay)
     def _():
-        gain_z[NQ - 1] = terms
-        lines = gain_z.at[pl.ds(0, NQ - 1)]
-        pltpu.make_async_copy(lines, lines, gz_recv).wait()
-        line = gain_z[0]
-        for qq in range(1, NQ):
-            line = line + gain_z[qq]
+        def wait_lines(count, sem):
+            lines = gain_z.at[pl.ds(0, count)]
+            pltpu.make_async_copy(lines, lines, sem).wait()
+
+        wait_lines(EARLY_Q - 1, gz_recv.at[0])
+        line = terms + gain_z[NQ - 2]
+        for n in range(EARLY_Q - 2):
+            line = line + gain_z[n]
+        gain_send[2] = line
+
+        @pl.when(starts_last)
+        def _():
+            for xx, qq, yy in FIRST:
+                remote(gain_send.at[2], gain_p.at[plane], gp_send, gp_recv, at(xx, qq, yy)).start()
+
+        wait_lines(NQ - EARLY_Q, gz_recv.at[1])
+        for n in range(EARLY_Q - 2, NQ - 2):
+            line = line + gain_z[n]
         gain_send[1] = line
         gain_p[plane] = line
         for dx, dy in AWAY:
-            device = at(lax.rem(x + dx, NX), 1, lax.rem(y + dy, NY))
-            remote(gain_send.at[1], gain_p.at[plane], gp_send, gp_recv, device).start()
-        remote(gain_send.at[1], gain_p.at[plane], gp_send, gp_recv, at(0, 3, 0)).start()
+            xx, yy = lax.rem(x + dx, NX), lax.rem(y + dy, NY)
+            first = jnp.logical_or(yy == 0, jnp.logical_and(xx == 0, yy == 1))
+
+            @pl.when(jnp.logical_not(jnp.logical_and(first, starts_last)))
+            def _(xx=xx, yy=yy):
+                remote(gain_send.at[1], gain_p.at[plane], gp_send, gp_recv, at(xx, 1, yy)).start()
+
+        @pl.when(jnp.logical_not(starts_last))
+        def _():
+            remote(gain_send.at[1], gain_p.at[plane], gp_send, gp_recv, at(0, 3, 0)).start()
 
     def gather(level, count):
         settle(count, xr_sem)
@@ -539,6 +577,17 @@
     def total_of_lines(senders):
         lines = gain_p.at[pl.ds(0, senders)]
         pltpu.make_async_copy(lines, lines, gp_recv).wait()
+
+        @pl.when(is_first)
+        def _():
+            pltpu.make_async_copy(gain_d, gain_d, gd_recv).wait()
+            for n in range(NX * len(LAST_Y)):
+                there = n // len(LAST_Y) * NY + LAST_Y[0] + n % len(LAST_Y)
+                line = gain_p[there]
+                for k in range(NQ - EARLY_Q):
+                    line = line + gain_d[n, k]
+                gain_p[there] = line
+
         total = gain_p[0]
         for n in range(1, NX * NY):
             total = total + gain_p[n]
@@ -588,6 +637,12 @@
     @pl.when(jnp.logical_not(is_relay))
     def _():
         pltpu.make_async_copy(gain_total, gain_total, gz_send).wait()
+
+        @pl.when(direct)
+        def _():
+            sent = gain_z.at[pl.ds(0, len(FIRST))]
+            pltpu.make_async_copy(sent, sent, gd_send).wait()
+
 
         @pl.when(jnp.logical_not(is_extra))
         def _():
@@ -662,9 +717,10 @@
             pltpu.VMEM((2, T, D), BF),
             pltpu.VMEM((2 * NX - 1, 2, T, D), BF),
             pltpu.VMEM((NQ, 2, T, D), BF),
-            pltpu.VMEM((2, 2, D), F32),
+            pltpu.VMEM((3, 2, D), F32),
             pltpu.VMEM((NQ, 2, D), F32),
             pltpu.VMEM((NX * NY, 2, D), F32),
+            pltpu.VMEM((NX * len(LAST_Y), NQ - EARLY_Q, 2, D), F32),
             pltpu.VMEM((2, D), F32),
             dma((8,)),
             dma(()),
@@ -674,6 +730,8 @@
             dma((2,)),
             dma(()),
             dma(()),
+            dma(()),
+            dma((2,)),
             dma(()),
             dma(()),
             dma(()),

time: 32.3 us -> 30.9 us (0.957)
  Pallas kernels: 30.8 us -> 29.4 us
    pallas_call x1, Pallas kernels: 30 us -> 28.6 us  [on_device(): pl.pallas_call(kernel, name='tree_backward', out_shape=[pltpu.VMEM(querie...]
where the time goes in v6:
time: 30.9 us; the launch traced here: 30.7 us
  Pallas kernels  29.4 us (95%)
  between operations  1.29 us (4%)
    pallas_call x1, Pallas kernels, on_device(): pl.pallas_call(kernel, name='tree_backward', out_shape=[pltpu.VMEM(querie...  28.6 us
    pallas_call x1, Pallas kernels, on_device(): pl.pallas_call(hand_over, name='hand_over', out_shape=[jax.ShapeDtypeStru...  0.76 us

profile of v6, /device:TPU:1, one launch (start us, length us, event | category | flops | bytes accessed | tf_op | source)
XLA Modules:
  0.0 30.7 jit_solution(321708777561083827)
XLA Ops:
  1.3 28.6 %tree_backward.1 = (bf16[2,64,1024]{2,1,0:T(8,128)(2,1)S(1)}, bf16[2,64,128]{2,1,0:T(8,128)(2,1)S(1)}, bf16[2,64,128]{2,1,0:T(8,128)(2,1)S(1)}, f32[1,128]{1,0:T(1,128)S(1)}, f32[1,128]{1,0:T(1,128)S(1)}) custom-call(bf16[2,64,1024]{2,1,0:T(8,128)(2,1)} %q_in.1, bf16[2,64,128]{2,1,0:T(8,128)(2,1)} %k_in.1, bf16[2,64,128]{2,1,0:T(8,128)(2,1)} %v_in.1, ...), custom_call_target="tpu_custom_call" | custom-call | flops 587202560 | bytes 1048576 | tf_op jit(solution)/shard_map/tree_backward/pallas_call | solution.py:680
  29.9 0.8 %hand_over.1 = (bf16[2,64,1024]{2,1,0:T(8,128)(2,1)}, bf16[2,64,128]{2,1,0:T(8,128)(2,1)}, bf16[2,64,128]{2,1,0:T(8,128)(2,1)}, f32[1,128]{1,0:T(1,128)}, f32[1,128]{1,0:T(1,128)}) custom-call(bf16[2,64,1024]{2,1,0:T(8,128)(2,1)S(1)} %get-tuple-element.15.refs_0_, bf16[2,64,128]{2,1,0:T(8,128)(2,1)S(1)} %get-tuple-element.16.refs_1_, ...), custom_call_target="tpu_custom_call" | custom-call | tf_op jit(solution)/shard_map/hand_over/pallas_call | solution.py:761

commit v7 on v6

--- a/solution.py
+++ b/solution.py
@@ -24,9 +24,9 @@
 BF = jnp.bfloat16
 F32 = jnp.float32
 MESH = pl.DeviceIdType.MESH
-FIRST = ((0, 1, 0), (0, 3, 0), (0, 1, 1), (1, 1, 0), (2, 1, 0), (3, 1, 0))
-LAST_Y = (4, 5)
-EARLY_Q = 6
+FIRST = ((0, 1, 0), (0, 3, 0), (0, 1, 1), (1, 1, 0), (0, 1, 2), (1, 1, 1), (2, 1, 0), (3, 1, 0))
+LAST_Y = (4,5,6)
+EARLY_Q = 4
 SERVED = ((1, (11, 13, 15, 3)), (5, (9, 7)))
 AWAY = sorted(
     ((dx, dy) for dx in range(NX) for dy in range(NY) if dx or dy),
@@ -100,7 +100,12 @@
     is_relay = q == 1
     is_near = q == 5
     is_extra = jnp.logical_and(leaf == 3, y == 0)
-    is_first = jnp.logical_or(is_extra, jnp.logical_and(is_relay, jnp.logical_or(y == 0, jnp.logical_and(x == 0, y == 1))))
+
+    def first_relay(xx, yy):
+        near_zero = jnp.logical_and(yy > 0, xx + yy < 3)
+        return jnp.logical_or(yy == 0, near_zero)
+
+    is_first = jnp.logical_or(is_extra, jnp.logical_and(is_relay, first_relay(x, y)))
     is_second = q == 9
     far_owner = jnp.logical_and(q == 0, x > 0)
     plane = x * NY + y
@@ -260,6 +265,12 @@
                 remote(own, kv.at[level], b_send, b_recv.at[level], at(x, 0)).wait_recv()
             for qq in (*served, relay - 1):
                 remote(top_two, top_two, b_send, b_recv.at[5], at(x, qq)).start()
+
+    @pl.when(q == 13)
+    def _():
+        remote(own, kv.at[3], b_send, b_recv.at[3], at(x, 12)).wait_recv()
+        for qq in (14, 15):
+            remote(kv.at[3], kv.at[3], b_send, b_recv.at[3], at(x, qq)).start()
 
     for load in loads[4:]:
         load.wait()
@@ -310,20 +321,14 @@
 
     @pl.when(q == 13)
     def _():
-        remote(own, kv.at[3], b_send, b_recv.at[3], at(x, 12)).wait_recv()
+        remote(own, kv.at[4], b_send, b_recv.at[4], at(x, 9)).wait_recv()
         for qq in (14, 15):
-            remote(kv.at[3], kv.at[3], b_send, b_recv.at[3], at(x, qq)).start()
+            remote(kv.at[4], kv.at[4], b_send, b_recv.at[4], at(x, qq)).start()
 
     take(0)
     for level in (1, 2):
         from_holder(level)
         take(level)
-
-    @pl.when(q == 13)
-    def _():
-        remote(own, kv.at[4], b_send, b_recv.at[4], at(x, 9)).wait_recv()
-        for qq in (14, 15):
-            remote(kv.at[4], kv.at[4], b_send, b_recv.at[4], at(x, qq)).start()
 
     @pl.when(jnp.logical_and(c == 1, jnp.logical_not(jnp.logical_or(is_relay, is_near))))
     def _():
@@ -503,7 +508,7 @@
         gain_p[plane] = line
         for dx, dy in AWAY:
             xx, yy = lax.rem(x + dx, NX), lax.rem(y + dy, NY)
-            first = jnp.logical_or(yy == 0, jnp.logical_and(xx == 0, yy == 1))
+            first = first_relay(xx, yy)
 
             @pl.when(jnp.logical_not(jnp.logical_and(first, starts_last)))
             def _(xx=xx, yy=yy):

time: 30.9 us -> 30.6 us (level)
  no operation moved by 1% of the time
where the time goes in v7:
time: 30.6 us; the launch traced here: 30.4 us
  Pallas kernels  29.1 us (95%)
  between operations  1.29 us (4%)
    pallas_call x1, Pallas kernels, on_device(): pl.pallas_call(kernel, name='tree_backward', out_shape=[pltpu.VMEM(querie...  28.3 us
    pallas_call x1, Pallas kernels, on_device(): pl.pallas_call(hand_over, name='hand_over', out_shape=[jax.ShapeDtypeStru...  0.76 us

profile of v7, /device:TPU:1, one launch (start us, length us, event | category | flops | bytes accessed | tf_op | source)
XLA Modules:
  0.0 30.4 jit_solution(13601526476742034525)
XLA Ops:
  1.3 28.3 %tree_backward.1 = (bf16[2,64,1024]{2,1,0:T(8,128)(2,1)S(1)}, bf16[2,64,128]{2,1,0:T(8,128)(2,1)S(1)}, bf16[2,64,128]{2,1,0:T(8,128)(2,1)S(1)}, f32[1,128]{1,0:T(1,128)S(1)}, f32[1,128]{1,0:T(1,128)S(1)}) custom-call(bf16[2,64,1024]{2,1,0:T(8,128)(2,1)} %q_in.1, bf16[2,64,128]{2,1,0:T(8,128)(2,1)} %k_in.1, bf16[2,64,128]{2,1,0:T(8,128)(2,1)} %v_in.1, ...), custom_call_target="tpu_custom_call" | custom-call | flops 587202560 | bytes 1048576 | tf_op jit(solution)/shard_map/tree_backward/pallas_call | solution.py:685
  29.6 0.8 %hand_over.1 = (bf16[2,64,1024]{2,1,0:T(8,128)(2,1)}, bf16[2,64,128]{2,1,0:T(8,128)(2,1)}, bf16[2,64,128]{2,1,0:T(8,128)(2,1)}, f32[1,128]{1,0:T(1,128)}, f32[1,128]{1,0:T(1,128)}) custom-call(bf16[2,64,1024]{2,1,0:T(8,128)(2,1)S(1)} %get-tuple-element.15.refs_0_, bf16[2,64,128]{2,1,0:T(8,128)(2,1)S(1)} %get-tuple-element.16.refs_1_, ...), custom_call_target="tpu_custom_call" | custom-call | tf_op jit(solution)/shard_map/hand_over/pallas_call | solution.py:766

commit v8 on v7

--- a/solution.py
+++ b/solution.py
@@ -15,8 +15,8 @@
 G = 8
 SLOTS = DEPTH + 1
 KEYS = SLOTS * T
-NEAR = 4
-MID = 5
+GROUPS = ((0, 3), (3, 5), (5, 6), (6, 7))
+
 ROWS = G * T
 NX, NZ, NC, NY = 4, 8, 2, 8
 NQ = NZ * NC
@@ -27,7 +27,7 @@
 FIRST = ((0, 1, 0), (0, 3, 0), (0, 1, 1), (1, 1, 0), (0, 1, 2), (1, 1, 1), (2, 1, 0), (3, 1, 0))
 LAST_Y = (4,5,6)
 EARLY_Q = 4
-SERVED = ((1, (11, 13, 15, 3)), (5, (9, 7)))
+SERVED = ((1, (11, 13, 15, 3)), (5, (8, 9, 7)))
 AWAY = sorted(
     ((dx, dy) for dx in range(NX) for dy in range(NY) if dx or dy),
     key=lambda step: -min(step[0], NX - step[0]) - min(step[1], NY - step[1]),
@@ -58,6 +58,12 @@
 def unit_of(x):
     factor = lax.rsqrt(jnp.mean(x * x, axis=-1, keepdims=True) + NORM_EPS)
     return x * factor, factor
+
+
+def tree_sum(terms):
+    while len(terms) > 1:
+        terms = [sum(terms[n + 1 : n + 2], terms[n]) for n in range(0, len(terms), 2)]
+    return terms[0]
 
 
 def dot(a, b, contract):
@@ -171,7 +177,7 @@
 
     early = jnp.where(c == 1, 1, 0)
     early = early + jnp.where(sends_six, 1, 0) + jnp.where(sends_five, 1, 0)
-    early = early + jnp.where(is_relay, 4 + NX * NY, 0) + jnp.where(is_near, 2 + jnp.where(starts_last, len(FIRST), 0), 0)
+    early = early + jnp.where(is_relay, 4 + NX * NY, 0) + jnp.where(is_near, 3 + jnp.where(starts_last, len(FIRST), 0), 0)
     early = early + jnp.where(is_second, 4, 0) + jnp.where(q == 13, 2, 0) - jnp.where(q == 12, 2, 0)
     for level, count in ((2, 3), (3, 7), (4, 9), (5, 4), (6, 2 * NX)):
         early = early + jnp.where(hosted == level, count, 0)
@@ -255,8 +261,6 @@
         for qq in (13, 12, 10, 11):
             remote(kv.at[4], kv.at[4], b_send, b_recv.at[4], at(x, qq)).start()
 
-    top_two = kv.at[pl.ds(5, 2)]
-
     for relay, served in SERVED:
 
         @pl.when(q == relay)
@@ -264,7 +268,8 @@
             for level in (5, 6):
                 remote(own, kv.at[level], b_send, b_recv.at[level], at(x, 0)).wait_recv()
             for qq in (*served, relay - 1):
-                remote(top_two, top_two, b_send, b_recv.at[5], at(x, qq)).start()
+                for level in (5, 6):
+                    remote(kv.at[level], kv.at[level], b_send, b_recv.at[level], at(x, qq)).start()
 
     @pl.when(q == 13)
     def _():
@@ -330,14 +335,6 @@
         from_holder(level)
         take(level)
 
-    @pl.when(jnp.logical_and(c == 1, jnp.logical_not(jnp.logical_or(is_relay, is_near))))
-    def _():
-        remote(top_two, top_two, b_send, b_recv.at[5], at(x, 1)).wait_recv()
-        remote(top_two, top_two, b_send, b_recv.at[5], at(x, q - 1)).start()
-
-    from_holder(3)
-    take(3)
-
     key_at = lax.broadcasted_iota(jnp.int32, (T, ROWS), 0)
     row_at = lax.rem(lax.broadcasted_iota(jnp.int32, (T, ROWS), 1), T)
     ahead = key_at - row_at
@@ -363,12 +360,13 @@
         top = jnp.max(scores, axis=0, keepdims=True)
         raised = jnp.exp(scores - top)
         dprobs = dot(v_all[slots, :], g_rows[rows, :], ((1,), (1,)))
+        products = raised * dprobs
         return (
             raised,
-            dprobs,
+            products,
             top,
             jnp.sum(raised, axis=0, keepdims=True),
-            jnp.sum(raised * dprobs, axis=0, keepdims=True),
+            jnp.sum(products, axis=0, keepdims=True),
         )
 
     def keep(first, last, at_row, kind, rows):
@@ -380,44 +378,67 @@
 
     for kind in range(2):
         rows = slice(kind * ROWS, (kind + 1) * ROWS)
-        keep(0, NEAR, 0, kind, rows)
-
+        keep(0, 3, 0, kind, rows)
+
+    @pl.when(jnp.logical_and(c == 1, jnp.logical_not(among((1, 5, 9)))))
+    def _():
+        for level in (5, 6):
+            remote(own, kv.at[level], b_send, b_recv.at[level], at(x, 1)).wait_recv()
+            remote(kv.at[level], kv.at[level], b_send, b_recv.at[level], at(x, q - 1)).start()
+
+    from_holder(3)
+    take(3)
     from_holder(4)
     take(4)
     for kind in range(2):
         rows = slice(kind * ROWS, (kind + 1) * ROWS)
-        keep(NEAR, MID, 3, kind, rows)
-
-    @pl.when(c == 0)
-    def _():
-        remote(top_two, top_two, b_send, b_recv.at[5], at(x, 1)).wait_recv()
-
+        keep(3, 5, 3, kind, rows)
+
+    def from_relay(level):
+        @pl.when(jnp.logical_or(c == 0, is_second))
+        def _():
+            remote(own, kv.at[level], b_send, b_recv.at[level], at(x, 1)).wait_recv()
+
+    from_relay(5)
     take(5)
-    take(6)
     for kind in range(2):
         rows = slice(kind * ROWS, (kind + 1) * ROWS)
-        far_e, far_d, far_top, far_sum, far_delta = partial(MID, SLOTS, kind)
-        near_top, mid_top = near_s[0:1, rows], near_s[3:4, rows]
-        top = jnp.maximum(jnp.maximum(near_top, mid_top), far_top)
-        near_f, mid_f, far_f = jnp.exp(near_top - top), jnp.exp(mid_top - top), jnp.exp(far_top - top)
-        over = 1.0 / (near_s[1:2, rows] * near_f + near_s[4:5, rows] * mid_f + far_sum * far_f)
-        near_f, mid_f, far_f = near_f * over, mid_f * over, far_f * over
-        delta = near_s[2:3, rows] * near_f + near_s[5:6, rows] * mid_f + far_delta * far_f
-        for first, last, factor, e, d in (
-            (0, NEAR, near_f, near_e[: NEAR * T, rows], near_d[: NEAR * T, rows]),
-            (NEAR, MID, mid_f, near_e[NEAR * T :, rows], near_d[NEAR * T :, rows]),
-            (MID, SLOTS, far_f, far_e, far_d),
-        ):
-            prob = e * factor
-            probs[first * T : last * T, rows] = prob.astype(BF)
-            dscores[first * T : last * T, rows] = (prob * (d - delta)).astype(BF)
+        keep(5, 6, 6, kind, rows)
+    from_relay(6)
+    take(6)
+
+    for kind in range(2):
+        rows = slice(kind * ROWS, (kind + 1) * ROWS)
+        last_e, last_d, *last = partial(SLOTS - 1, SLOTS, kind)
+        sums = [[near_s[3 * n + line : 3 * n + line + 1, rows] for line in range(3)] for n in range(len(GROUPS) - 1)]
+        sums.append(last)
+        top = sums[0][0]
+        for group in sums[1:]:
+            top = jnp.maximum(top, group[0])
+        factors = [jnp.exp(group[0] - top) for group in sums]
+        total = sums[0][1] * factors[0]
+        delta = sums[0][2] * factors[0]
+        for group, factor in zip(sums[1:], factors[1:]):
+            total = total + group[1] * factor
+            delta = delta + group[2] * factor
+        over = 1.0 / total
+        delta = delta * over
+        for n, (first, after) in enumerate(GROUPS):
+            here = slice(first * T, after * T)
+            e, d = (last_e, last_d) if n == len(GROUPS) - 1 else (near_e[here, rows], near_d[here, rows])
+            factor = factors[n] * over
+            dscores[here, rows] = (d * factor - e * (factor * delta)).astype(BF)
+            near_s[n : n + 1, rows] = factor
+        near_e[(SLOTS - 1) * T :, rows] = last_e
     dk_all = dot(dscores[...], q_rot[...], ((1,), (0,))) * SCALE
     dq_turned = dot(k_rot[...], dscores[...], ((0,), (0,))) * SCALE
-    straight, crossed = dq_turned * wq_cos[...], dq_turned * wq_sin[...]
-    both = straight - jnp.concatenate([crossed[D // 2 :], crossed[: D // 2]], axis=0)
-    lanes = both[:, :D]
-    for n in range(1, 2 * ROWS // D):
-        lanes = lanes + both[:, n * D : (n + 1) * D]
+    lanes, crossed = None, None
+    for n in range(2 * ROWS // D):
+        tile = slice(n * D, (n + 1) * D)
+        one, other = dq_turned[:, tile] * wq_cos[:, tile], dq_turned[:, tile] * wq_sin[:, tile]
+        lanes = one if lanes is None else lanes + one
+        crossed = other if crossed is None else crossed + other
+    lanes = lanes - jnp.concatenate([crossed[D // 2 :], crossed[: D // 2]], axis=0)
     gain_q = jnp.sum(jnp.transpose(lanes), axis=0, keepdims=True)
     gain_k = jnp.sum(dk_all * wk_cos[...], axis=0, keepdims=True) - pltpu.roll(
         jnp.sum(dk_all * wk_sin[...], axis=0, keepdims=True), D // 2, axis=1
@@ -436,6 +457,9 @@
         recv = gz_recv.at[jnp.where(q < EARLY_Q, 0, 1)]
         remote(gain_send.at[0], gain_z.at[lax.rem(q + NQ - 2, NQ)], gz_send, recv, at(x, 1)).start()
 
+    for n, (first, after) in enumerate(GROUPS):
+        here = slice(first * T, after * T)
+        probs[here, :] = (near_e[here, :] * near_s[n : n + 1, :]).astype(BF)
     dv_all = dot(probs[...], g_rows[...], ((1,), (0,)))
     for slot in range(SLOTS):
         part[slot, 0] = dk_all[slot * T : (slot + 1) * T]
@@ -461,6 +485,23 @@
             n = lax.rem(q, 2**level)
             n = jnp.where(n > 2 ** (level - 1), n - 1, n)
             remote(send_kv.at[level - 1], z_recv.at[n], r_send, r_recv, at(x, holder[level])).start()
+
+    def wait_lines(count, sem):
+        lines = gain_z.at[pl.ds(0, count)]
+        pltpu.make_async_copy(lines, lines, sem).wait()
+
+    @pl.when(is_relay)
+    def _():
+        wait_lines(EARLY_Q - 1, gz_recv.at[0])
+        line = terms + gain_z[NQ - 2]
+        for n in range(EARLY_Q - 2):
+            line = line + gain_z[n]
+        gain_send[2] = line
+
+        @pl.when(starts_last)
+        def _():
+            for xx, qq, yy in FIRST:
+                remote(gain_send.at[2], gain_p.at[plane], gp_send, gp_recv, at(xx, qq, yy)).start()
 
     y_q[...] = jnp.transpose(dq_turned)
     for kind in range(2):
@@ -486,24 +527,9 @@
 
     @pl.when(is_relay)
     def _():
-        def wait_lines(count, sem):
-            lines = gain_z.at[pl.ds(0, count)]
-            pltpu.make_async_copy(lines, lines, sem).wait()
-
-        wait_lines(EARLY_Q - 1, gz_recv.at[0])
-        line = terms + gain_z[NQ - 2]
-        for n in range(EARLY_Q - 2):
-            line = line + gain_z[n]
-        gain_send[2] = line
-
-        @pl.when(starts_last)
-        def _():
-            for xx, qq, yy in FIRST:
-                remote(gain_send.at[2], gain_p.at[plane], gp_send, gp_recv, at(xx, qq, yy)).start()
-
+        line = gain_send[2]
         wait_lines(NQ - EARLY_Q, gz_recv.at[1])
-        for n in range(EARLY_Q - 2, NQ - 2):
-            line = line + gain_z[n]
+        line = line + tree_sum([gain_z[n] for n in range(EARLY_Q - 2, NQ - 2)])
         gain_send[1] = line
         gain_p[plane] = line
         for dx, dy in AWAY:
@@ -540,7 +566,7 @@
     def _():
         remote(send_sum, z_recv.at[q - 1], s_send, r_recv, at(x, 0)).start()
 
-    for places, count in (((1,), 11), ((5, 9, 13), 7), ((4,), 7), ((12,), 5)):
+    for places, count in (((1,), 11), ((5,), 9), ((9,), 5), ((13,), 7), ((4,), 7), ((12,), 5)):
 
         @pl.when(among(places))
         def _(count=count):
@@ -579,24 +605,21 @@
         dk_out[1] = jnp.zeros((T, D), BF)
         dv_out[1] = jnp.zeros((T, D), BF)
 
-    def total_of_lines(senders):
+    last_lines = [xx * NY + yy for xx in range(NX) for yy in LAST_Y]
+
+    def total_of_lines(senders, straight):
         lines = gain_p.at[pl.ds(0, senders)]
         pltpu.make_async_copy(lines, lines, gp_recv).wait()
-
-        @pl.when(is_first)
-        def _():
+        others = tree_sum([gain_p[n] for n in range(NX * NY) if n not in last_lines])
+        if straight:
             pltpu.make_async_copy(gain_d, gain_d, gd_recv).wait()
-            for n in range(NX * len(LAST_Y)):
-                there = n // len(LAST_Y) * NY + LAST_Y[0] + n % len(LAST_Y)
-                line = gain_p[there]
-                for k in range(NQ - EARLY_Q):
-                    line = line + gain_d[n, k]
-                gain_p[there] = line
-
-        total = gain_p[0]
-        for n in range(1, NX * NY):
-            total = total + gain_p[n]
-        gain_total[...] = total
+        late = []
+        for n, there in enumerate(last_lines):
+            line = gain_p[there]
+            if straight:
+                line = line + tree_sum([gain_d[n, k] for k in range(NQ - EARLY_Q)])
+            late.append(line)
+        gain_total[...] = others + tree_sum(late)
 
     def pass_on(when, targets):
         @pl.when(when)
@@ -604,13 +627,17 @@
             for qq in targets:
                 remote(gain_total, gain_total, gt_send, gt_recv, at(x, qq)).start()
 
-    @pl.when(is_relay)
-    def _():
-        total_of_lines(NX * NY - 1)
+    @pl.when(jnp.logical_and(is_relay, is_first))
+    def _():
+        total_of_lines(NX * NY - 1, True)
+
+    @pl.when(jnp.logical_and(is_relay, jnp.logical_not(is_first)))
+    def _():
+        total_of_lines(NX * NY - 1, False)
 
     @pl.when(is_extra)
     def _():
-        total_of_lines(NX * NY)
+        total_of_lines(NX * NY, True)
 
     pass_on(jnp.logical_and(is_relay, plane > 0), (3, 5, 7, 0))
     pass_on(is_extra, (5, 7, 2, 0))
@@ -710,9 +737,9 @@
             pltpu.VMEM((D, 2 * ROWS), F32),
             pltpu.VMEM((KEYS, D), F32),
             pltpu.VMEM((KEYS, D), F32),
-            pltpu.VMEM((MID * T, 2 * ROWS), F32),
-            pltpu.VMEM((MID * T, 2 * ROWS), F32),
-            pltpu.VMEM((8, 2 * ROWS), F32),
+            pltpu.VMEM((KEYS, 2 * ROWS), F32),
+            pltpu.VMEM(((SLOTS - 1) * T, 2 * ROWS), F32),
+            pltpu.VMEM((16, 2 * ROWS), F32),
             pltpu.VMEM((KEYS, 2 * ROWS), BF),
             pltpu.VMEM((KEYS, 2 * ROWS), BF),
             pltpu.VMEM((SLOTS, 2, T, D), F32),

time: 30.6 us -> 30.6 us (level)
  no operation moved by 1% of the time
where the time goes in v8:
time: 30.6 us; the launch traced here: 30.4 us
  Pallas kernels  29.1 us (95%)
  between operations  1.29 us (4%)
    pallas_call x1, Pallas kernels, on_device(): pl.pallas_call(kernel, name='tree_backward', out_shape=[pltpu.VMEM(querie...  28.3 us
    pallas_call x1, Pallas kernels, on_device(): pl.pallas_call(hand_over, name='hand_over', out_shape=[jax.ShapeDtypeStru...  0.76 us

profile of v8, /device:TPU:1, one launch (start us, length us, event | category | flops | bytes accessed | tf_op | source)
XLA Modules:
  0.0 30.4 jit_solution(17292096322385249385)
XLA Ops:
  1.3 28.3 %tree_backward.1 = (bf16[2,64,1024]{2,1,0:T(8,128)(2,1)S(1)}, bf16[2,64,128]{2,1,0:T(8,128)(2,1)S(1)}, bf16[2,64,128]{2,1,0:T(8,128)(2,1)S(1)}, f32[1,128]{1,0:T(1,128)S(1)}, f32[1,128]{1,0:T(1,128)S(1)}) custom-call(bf16[2,64,1024]{2,1,0:T(8,128)(2,1)} %q_in.1, bf16[2,64,128]{2,1,0:T(8,128)(2,1)} %k_in.1, bf16[2,64,128]{2,1,0:T(8,128)(2,1)} %v_in.1, ...), custom_call_target="tpu_custom_call" | custom-call | flops 587202560 | bytes 1048576 | tf_op jit(solution)/shard_map/tree_backward/pallas_call | solution.py:712
  29.6 0.8 %hand_over.1 = (bf16[2,64,1024]{2,1,0:T(8,128)(2,1)}, bf16[2,64,128]{2,1,0:T(8,128)(2,1)}, bf16[2,64,128]{2,1,0:T(8,128)(2,1)}, f32[1,128]{1,0:T(1,128)}, f32[1,128]{1,0:T(1,128)}) custom-call(bf16[2,64,1024]{2,1,0:T(8,128)(2,1)S(1)} %get-tuple-element.15.refs_0_, bf16[2,64,128]{2,1,0:T(8,128)(2,1)S(1)} %get-tuple-element.16.refs_1_, ...), custom_call_target="tpu_custom_call" | custom-call | tf_op jit(solution)/shard_map/hand_over/pallas_call | solution.py:793

commit v9 on v8

--- a/solution.py
+++ b/solution.py
@@ -15,7 +15,7 @@
 G = 8
 SLOTS = DEPTH + 1
 KEYS = SLOTS * T
-GROUPS = ((0, 3), (3, 5), (5, 6), (6, 7))
+GROUPS = ((0, 3), (3, 5), (5, 7))
 
 ROWS = G * T
 NX, NZ, NC, NY = 4, 8, 2, 8
@@ -401,15 +401,12 @@
 
     from_relay(5)
     take(5)
+    from_relay(6)
+    take(6)
+
     for kind in range(2):
         rows = slice(kind * ROWS, (kind + 1) * ROWS)
-        keep(5, 6, 6, kind, rows)
-    from_relay(6)
-    take(6)
-
-    for kind in range(2):
-        rows = slice(kind * ROWS, (kind + 1) * ROWS)
-        last_e, last_d, *last = partial(SLOTS - 1, SLOTS, kind)
+        last_e, last_d, *last = partial(GROUPS[-1][0], SLOTS, kind)
         sums = [[near_s[3 * n + line : 3 * n + line + 1, rows] for line in range(3)] for n in range(len(GROUPS) - 1)]
         sums.append(last)
         top = sums[0][0]
@@ -429,7 +426,7 @@
             factor = factors[n] * over
             dscores[here, rows] = (d * factor - e * (factor * delta)).astype(BF)
             near_s[n : n + 1, rows] = factor
-        near_e[(SLOTS - 1) * T :, rows] = last_e
+        near_e[GROUPS[-1][0] * T :, rows] = last_e
     dk_all = dot(dscores[...], q_rot[...], ((1,), (0,))) * SCALE
     dq_turned = dot(k_rot[...], dscores[...], ((0,), (0,))) * SCALE
     lanes, crossed = None, None

time: 30.6 us -> 30.5 us (level)
  no operation moved by 1% of the time
where the time goes in v9:
time: 30.5 us; the launch traced here: 30.3 us
  Pallas kernels  29 us (95%)
  between operations  1.29 us (4%)
    pallas_call x1, Pallas kernels, on_device(): pl.pallas_call(kernel, name='tree_backward', out_shape=[pltpu.VMEM(querie...  28.2 us
    pallas_call x1, Pallas kernels, on_device(): pl.pallas_call(hand_over, name='hand_over', out_shape=[jax.ShapeDtypeStru...  0.76 us

profile of v9, /device:TPU:1, one launch (start us, length us, event | category | flops | bytes accessed | tf_op | source)
XLA Modules:
  0.0 30.3 jit_solution(11180551842387768620)
XLA Ops:
  1.3 28.2 %tree_backward.1 = (bf16[2,64,1024]{2,1,0:T(8,128)(2,1)S(1)}, bf16[2,64,128]{2,1,0:T(8,128)(2,1)S(1)}, bf16[2,64,128]{2,1,0:T(8,128)(2,1)S(1)}, f32[1,128]{1,0:T(1,128)S(1)}, f32[1,128]{1,0:T(1,128)S(1)}) custom-call(bf16[2,64,1024]{2,1,0:T(8,128)(2,1)} %q_in.1, bf16[2,64,128]{2,1,0:T(8,128)(2,1)} %k_in.1, bf16[2,64,128]{2,1,0:T(8,128)(2,1)} %v_in.1, ...), custom_call_target="tpu_custom_call" | custom-call | flops 587202560 | bytes 1048576 | tf_op jit(solution)/shard_map/tree_backward/pallas_call | solution.py:709
  29.5 0.8 %hand_over.1 = (bf16[2,64,1024]{2,1,0:T(8,128)(2,1)}, bf16[2,64,128]{2,1,0:T(8,128)(2,1)}, bf16[2,64,128]{2,1,0:T(8,128)(2,1)}, f32[1,128]{1,0:T(1,128)}, f32[1,128]{1,0:T(1,128)}) custom-call(bf16[2,64,1024]{2,1,0:T(8,128)(2,1)S(1)} %get-tuple-element.15.refs_0_, bf16[2,64,128]{2,1,0:T(8,128)(2,1)S(1)} %get-tuple-element.16.refs_1_, ...), custom_call_target="tpu_custom_call" | custom-call | tf_op jit(solution)/shard_map/hand_over/pallas_call | solution.py:790

commit v10 on v9

--- a/solution.py
+++ b/solution.py
@@ -25,7 +25,7 @@
 F32 = jnp.float32
 MESH = pl.DeviceIdType.MESH
 FIRST = ((0, 1, 0), (0, 3, 0), (0, 1, 1), (1, 1, 0), (0, 1, 2), (1, 1, 1), (2, 1, 0), (3, 1, 0))
-LAST_Y = (4,5,6)
+LAST_Y = (3,4,5,6)
 EARLY_Q = 4
 SERVED = ((1, (11, 13, 15, 3)), (5, (8, 9, 7)))
 AWAY = sorted(

time: 30.5 us -> 30.5 us (level)
  no operation moved by 1% of the time
where the time goes in v10:
time: 30.5 us; the launch traced here: 30.3 us
  Pallas kernels  29 us (95%)
  between operations  1.29 us (4%)
    pallas_call x1, Pallas kernels, on_device(): pl.pallas_call(kernel, name='tree_backward', out_shape=[pltpu.VMEM(querie...  28.3 us
    pallas_call x1, Pallas kernels, on_device(): pl.pallas_call(hand_over, name='hand_over', out_shape=[jax.ShapeDtypeStru...  0.76 us

profile of v10, /device:TPU:1, one launch (start us, length us, event | category | flops | bytes accessed | tf_op | source)
XLA Modules:
  0.0 30.3 jit_solution(15037469842447187342)
XLA Ops:
  1.3 28.3 %tree_backward.1 = (bf16[2,64,1024]{2,1,0:T(8,128)(2,1)S(1)}, bf16[2,64,128]{2,1,0:T(8,128)(2,1)S(1)}, bf16[2,64,128]{2,1,0:T(8,128)(2,1)S(1)}, f32[1,128]{1,0:T(1,128)S(1)}, f32[1,128]{1,0:T(1,128)S(1)}) custom-call(bf16[2,64,1024]{2,1,0:T(8,128)(2,1)} %q_in.1, bf16[2,64,128]{2,1,0:T(8,128)(2,1)} %k_in.1, bf16[2,64,128]{2,1,0:T(8,128)(2,1)} %v_in.1, ...), custom_call_target="tpu_custom_call" | custom-call | flops 587202560 | bytes 1048576 | tf_op jit(solution)/shard_map/tree_backward/pallas_call | solution.py:709
  29.5 0.8 %hand_over.1 = (bf16[2,64,1024]{2,1,0:T(8,128)(2,1)}, bf16[2,64,128]{2,1,0:T(8,128)(2,1)}, bf16[2,64,128]{2,1,0:T(8,128)(2,1)}, f32[1,128]{1,0:T(1,128)}, f32[1,128]{1,0:T(1,128)}) custom-call(bf16[2,64,1024]{2,1,0:T(8,128)(2,1)S(1)} %get-tuple-element.15.refs_0_, bf16[2,64,128]{2,1,0:T(8,128)(2,1)S(1)} %get-tuple-element.16.refs_1_, ...), custom_call_target="tpu_custom_call" | custom-call | tf_op jit(solution)/shard_map/hand_over/pallas_call | solution.py:790
